TPU v7x, 256 devices: a whole 4x4x8 slice. The times are simulated.
256 devices in a mesh: mem: 4 (over z_hi), lat: 64 (over x, z_lo, y, core).
Axes of the slice: x: 4, y: 4, z: 8 (z_hi: 4, z_lo: 2; z = z_hi * 2 + z_lo), core: 2. Of those that a mesh axis runs over, the one named last changes fastest.
Arguments:
- members: float32 [32, 2, 512, 1024], P('mem', None, 'lat'), may hold values from -0.75 to 0.75
- lat_root: float32 [512, 512], replicated, may hold values from -1 to 2
- lon_root: float32 [1024, 1024], replicated, may hold values from -1 to 2
- innovation: float32 [512, 256], P('lat', 'mem'), may hold values from -6 to 6
- obs_weight: float32 [512, 256], P('lat', 'mem'), may hold values from 0.5 to 4
- obs_mask: int32 [512, 256], P('lat', 'mem'), may hold values 0 or 1
- obs_cell: int32 [512, 256], P('lat', 'mem'), may hold values from 0 to 2047, as said below
Outputs:
- increment: float32 [2, 512, 1024], P(None, 'lat', 'mem')
- control: float32 [32, 2, 512, 1024], P('mem', None, 'lat')
Inputs may be any that keep to these rules, and one draw needn't show every extreme that they name: `obs_cell`: entry e in column c has (e % 1024) // 256 equal to c // 64.
All inputs are finite; a program needn't handle non-finite values. No bound on the sum of `obs_mask` on one device may be relied on, other than what follows from the above.
Results may differ from a plain program's by a relative error of at most 0.0003.
Values sent between devices are 32-bit elements; how exact they have to be, the bound alone decides.
A program may use at most 64 MiB of HBM per device.

v0:
```python
import jax
import jax.numpy as jnp
from jax import lax
from jax.sharding import Mesh
from jax.sharding import PartitionSpec as P

LON_BLOCK = 128
INNER = 2
LAT = ("lat_0", "lat_1", "lat_2", "lat_3")
MEM_LAT = ("mem", "lat_0", "lat_1", "lat_2", "lat_3")


HIGH = lax.Precision.HIGHEST


def in_blocks(shard, dim, count):
    dims = shard.shape
    tiles = shard.reshape(*dims[:dim], count, dims[dim] // count, *dims[dim + 1 :])
    return jnp.moveaxis(tiles, dim, 0)


def summed_on_arrival(shard, axis, dim):
    tiles = in_blocks(shard, dim, lax.axis_size(axis))
    arrived = lax.all_to_all(tiles, axis, split_axis=0, concat_axis=0, tiled=True)
    return arrived.sum(axis=0)


def joined_along(tiles, dim):
    tiles = jnp.moveaxis(tiles, 0, dim)
    dims = tiles.shape
    return tiles.reshape(*dims[:dim], dims[dim] * dims[dim + 1], *dims[dim + 2 :])


def from_everyone(shard, axis):
    count = lax.axis_size(axis)
    return lax.all_to_all(
        jnp.broadcast_to(shard[None], (count, *shard.shape)), axis, 0, 0, tiled=True
    )


def gathered_copies(shard, axis, dim):
    return joined_along(from_everyone(shard, axis), dim)


def by_axis(shard, axes):
    for axis in axes:
        shard = lax.psum(shard, axis)
    return shard


def per_device(members, lat_root, lon_root, innovation, obs_weight, obs_mask, obs_cell):
    mem_dev, levels, rows, nlon = members.shape
    nblocks = nlon // LON_BLOCK
    fields = mem_dev * levels
    quarter = nlon // lax.axis_size("mem")
    lon_pair = lon_root.reshape(nlon, nblocks, LON_BLOCK)
    weights = obs_weight * obs_mask.astype(jnp.float32)
    local_cell = obs_cell // nlon * quarter + obs_cell % nlon - lax.axis_index("mem") * quarter
    row_ids = jnp.broadcast_to(jnp.arange(rows, dtype=jnp.int32)[:, None], obs_cell.shape)

    def to_strips(blocked):
        return lax.all_to_all(blocked, LAT, split_axis=0, concat_axis=1, tiled=True)

    def to_rows(strips):
        return lax.all_to_all(strips, LAT, split_axis=1, concat_axis=0, tiled=True)

    def latitude(strips, adjoint):
        form = "ji,pjc->pic" if adjoint else "ij,pjc->pic"
        return jnp.einsum(form, lat_root, strips, precision=HIGH)

    def lon_adjoint(field):
        blocked = jnp.einsum("frn,nbc->fbrc", field, lon_pair, precision=HIGH)
        return blocked.reshape(fields * nblocks, rows, LON_BLOCK)

    def adjoint(field):
        return latitude(to_strips(lon_adjoint(field)), True)

    def spread(values):
        flat = jnp.zeros((rows, levels * quarter), jnp.float32).at[row_ids, local_cell].add(values)
        field = flat.reshape(rows, levels, quarter).transpose(1, 0, 2)
        whole = gathered_copies(field, "mem", 2)
        return adjoint((members * whole[None]).reshape(fields, rows, nlon))

    def squares(vector):
        return by_axis(jnp.sum(vector * vector), MEM_LAT)

    gradient = spread(-(weights * innovation))
    control = jnp.zeros_like(gradient)
    increment = jnp.zeros((levels, rows, quarter), jnp.float32)
    norm_now = squares(gradient)
    for step in range(INNER):
        lon_shaped = to_rows(latitude(gradient, False)).reshape(fields, nblocks, rows, LON_BLOCK)
        partial_value = jnp.sum(
            members
            * jnp.einsum("fbrc,nbc->frn", lon_shaped, lon_pair, precision=HIGH).reshape(
                mem_dev, levels, rows, nlon
            ),
            axis=0,
        )
        image = summed_on_arrival(partial_value, "mem", 2)
        observe_flat = image.transpose(1, 0, 2).reshape(rows, levels * quarter)
        curved = gradient + spread(weights * jnp.take_along_axis(observe_flat, local_cell, axis=1))
        length = norm_now / by_axis(jnp.sum(gradient * curved), MEM_LAT)
        control = control - length * gradient
        increment = increment - length * image
        gradient = gradient - length * curved
        if step + 1 < INNER:
            norm_now = squares(gradient)
    shaped = to_rows(control).reshape(fields, nblocks, rows, LON_BLOCK).transpose(0, 2, 1, 3)
    control = shaped.reshape(fields, rows, nlon)
    return (increment, control.reshape(mem_dev, levels, rows, nlon))


def solution(mesh):
    finer = Mesh(
        mesh.devices.reshape(mesh.shape["mem"], 4, 2, 4, 2),
        ("mem", "lat_0", "lat_1", "lat_2", "lat_3"),
    )
    placed = (
        P("mem", None, LAT, None),
        P(),
        P(),
        P(LAT, "mem"),
        P(LAT, "mem"),
        P(LAT, "mem"),
        P(LAT, "mem"),
    )
    return jax.shard_map(
        per_device,
        mesh=finer,
        in_specs=placed,
        out_specs=(P(None, LAT, "mem"), P("mem", None, LAT, None)),
        check_vma=False,
    )
```

profile of v0, /device:TPU:1, one launch (start us, length us, event | category | flops | bytes accessed | tf_op | source)
XLA Modules:
  0.0 367.9 jit_solution(17815400289269395363)
XLA Ops:
  0.6 0.8 fusion.46
  1.5 0.7 multiply_negate_fusion
  2.3 23.9 %scatter_fusion = f32[8,512]{1,0:T(8,128)S(1)} fusion(f32[8,512]{1,0:T(8,128)S(1)} %broadcast.43.clone, s32[512]{0:T(512)S(1)} %reshape.118, f32[512]{0:T(512)S(1)} %reshape.120), kind=kCustom, calls=%fused_computation.2 | custom fusion | flops 512 | bytes 10240 | tf_op jit(solution)/shard_map/scatter-add | solution.py:79
  26.3 15.8 %all_to_all.124 = f32[4,2,8,256]{3,2,1,0:T(8,128)S(1)} all-to-all(f32[4,2,8,256]{3,2,1,0:T(8,128)S(1)} %broadcast_in_dim.20), channel_id=1, replica_groups=mesh['mem'=4,'lat_0'=4,'lat_1'=2,'lat_2'=4,'lat_3'=2] {'mem'}, dimensions={0} | all-to-all | bytes 131072 | tf_op jit(solution)/shard_map/all_to_all | solution.py:36
  42.2 4.6 %fusion.2 = f32[16,8,8,128]{3,1,2,0:T(8,128)S(1)} fusion(f32[16,8,1024,1]{2,1,3,0:T(8,128)S(1)} %bitcast.204, f32[1024,1024]{1,0:T(8,128)} %param.11), kind=kOutput, calls=%fused_computation.8 | convolution fusion | flops 1610612736 | bytes 5242880 | tf_op jit(solution)/shard_map/frn,nbc->fbrc/dot_general | solution.py:72
  46.8 22.3 %all_to_all.125 = f32[128,8,128]{2,1,0:T(8,128)S(1)} all-to-all(f32[128,8,128]{2,1,0:T(8,128)S(1)} %bitcast.205), channel_id=1, replica_groups=mesh['mem'=4,'lat_0'=4,'lat_1'=2,'lat_2'=4,'lat_3'=2] {'lat_0','lat_1','..., dimensions={0} | all-to-all | bytes 1048576 | tf_op jit(solution)/shard_map/all_to_all | solution.py:62
  69.1 1.1 convolution_bitcast_fusion.4
  70.2 1.1 convolution_bitcast_fusion.3
  71.2 1.0 copy.72
  72.2 4.6 %all-to-all-start.2 = ((f32[2,512,128]{2,0,1:T(2,128)}), f32[2,512,128]{2,0,1:T(2,128)S(1)}, u32[]{:S(2)}, u32[]{:S(2)}) async-start(f32[2,512,128]{2,0,1:T(2,128)} %copy.72), calls=%async_computation.2 | async-start | bytes 1048576 | tf_op jit(solution)/shard_map/all_to_all | solution.py:65
  76.9 5.1 %copy.111 = f32[128,8,8,128]{3,2,1,0:T(8,128)} copy(f32[128,8,8,128]{3,1,2,0:T(8,128)} %bitcast.200) | data formatting | bytes 8388608
  82.0 7.3 %all-to-all-done.2 = f32[2,512,128]{2,0,1:T(2,128)S(1)} async-done(((f32[2,512,128]{2,0,1:T(2,128)}), f32[2,512,128]{2,0,1:T(2,128)S(1)}, u32[]{:S(2)}, u32[]{:S(2)}) %all-to-all-start.2) | async-done | bytes 524320 | tf_op jit(solution)/shard_map/all_to_all | solution.py:65
  89.4 6.8 %fusion.25 = f32[2,8,1024]{2,1,0:T(8,128)S(1)} fusion(f32[8,2,8,1024]{3,2,1,0:T(8,128)S(1)} %copy-done.1, f32[8,2,8,8,128]{4,2,3,1,0:T(8,128)S(1)} %bitcast.217, f32[1024,8,128,1,1]{2,1,0,4,3:T(8,128)} %bitcast.201), kind=kOutput, calls=%fused_computation.28 | convolution fusion | flops 1610858496 | bytes 5308416 | tf_op jit(solution)/shard_map/fbrc,nbc->frn/dot_general | solution.py:95
  96.3 0.6 copy.76
  97.0 3.3 all-to-all-start.3
  100.3 6.8 %all-to-all-done.3 = f32[4,2,8,256]{3,2,1,0:T(8,128)S(1)} async-done(((f32[4,2,8,256]{3,2,1,0:T(8,128)}), f32[4,2,8,256]{3,2,1,0:T(8,128)S(1)}, u32[]{:S(2)}, u32[]{:S(2)}) %all-to-all-start.3) | async-done | bytes 65568 | tf_op jit(solution)/shard_map/all_to_all | solution.py:24
  107.1 3.6 gather_fusion
  110.9 23.9 %scatter_fusion.1 = f32[8,512]{1,0:T(8,128)S(1)} fusion(f32[8,512]{1,0:T(8,128)S(1)} %broadcast.43.clone.1, s32[512]{0:T(512)S(1)} %reshape.118, f32[512]{0:T(512)S(1)} %reshape.126), kind=kCustom, calls=%fused_computation.3 | custom fusion | flops 512 | bytes 10240 | tf_op jit(solution)/shard_map/scatter-add | solution.py:79
  134.8 9.3 %all_to_all.126 = f32[4,2,8,256]{3,2,1,0:T(8,128)S(1)} all-to-all(f32[4,2,8,256]{3,2,1,0:T(8,128)S(1)} %broadcast_in_dim.21), channel_id=1, replica_groups=mesh['mem'=4,'lat_0'=4,'lat_1'=2,'lat_2'=4,'lat_3'=2] {'mem'}, dimensions={0} | all-to-all | bytes 131072 | tf_op jit(solution)/shard_map/all_to_all | solution.py:36
  144.2 4.6 %fusion.1 = f32[16,8,8,128]{3,1,2,0:T(8,128)S(1)} fusion(f32[16,8,1024,1]{2,1,3,0:T(8,128)S(1)} %bitcast.206, f32[1024,1024]{1,0:T(8,128)} %param.11), kind=kOutput, calls=%fused_computation.7 | convolution fusion | flops 1610612736 | bytes 5242880 | tf_op jit(solution)/shard_map/frn,nbc->fbrc/dot_general | solution.py:72
  148.8 19.5 %all_to_all.127 = f32[128,8,128]{2,1,0:T(8,128)S(1)} all-to-all(f32[128,8,128]{2,1,0:T(8,128)S(1)} %bitcast.207), channel_id=1, replica_groups=mesh['mem'=4,'lat_0'=4,'lat_1'=2,'lat_2'=4,'lat_3'=2] {'lat_0','lat_1','..., dimensions={0} | all-to-all | bytes 1048576 | tf_op jit(solution)/shard_map/all_to_all | solution.py:62
  168.3 1.8 multiply_reduce_fusion.1
  170.1 7.8 %all-reduce.5 = (f32[]{:T(128)}, f32[]{:T(128)}) all-reduce(f32[]{:T(128)} %get-tuple-element.4, f32[]{:T(128)} %get-tuple-element.3), channel_id=1, replica_groups=mesh['mem'=4,'lat_0'=4,'lat_1'=2,'lat_2'=4,'lat_3'=2] {'mem'}, use_global_device_ids=true, to_apply=%region_2.3 | all-reduce | flops 2 | bytes 16 | tf_op jit(solution)/shard_map/psum | solution.py:47
  177.9 7.4 %all-reduce.3 = (f32[]{:T(128)}, f32[]{:T(128)}) all-reduce(f32[]{:T(128)} %get-tuple-element.15, f32[]{:T(128)} %get-tuple-element.16), channel_id=1, replica_groups=mesh['mem'=4,'lat_0'=4,'lat_1'=2,'lat_2'=4,'lat_3'=2] {'lat_0'}, use_global_device_ids=true, to_apply=%region_3.4 | all-reduce | flops 2 | bytes 16 | tf_op jit(solution)/shard_map/psum | solution.py:47
  185.3 4.4 %all-reduce.9 = (f32[]{:T(128)}, f32[]{:T(128)}) all-reduce(f32[]{:T(128)} %get-tuple-element.11, f32[]{:T(128)} %get-tuple-element.12), channel_id=1, replica_groups=mesh['mem'=4,'lat_0'=4,'lat_1'=2,'lat_2'=4,'lat_3'=2] {'lat_1'}, use_global_device_ids=true, to_apply=%region_4.5 | all-reduce | flops 2 | bytes 16 | tf_op jit(solution)/shard_map/psum | solution.py:47
  189.7 7.1 %all-reduce.1 = (f32[]{:T(128)}, f32[]{:T(128)}) all-reduce(f32[]{:T(128)} %get-tuple-element.23, f32[]{:T(128)} %get-tuple-element.24), channel_id=1, replica_groups=mesh['mem'=4,'lat_0'=4,'lat_1'=2,'lat_2'=4,'lat_3'=2] {'lat_2'}, use_global_device_ids=true, to_apply=%region_5.6 | all-reduce | flops 2 | bytes 16 | tf_op jit(solution)/shard_map/psum | solution.py:47
  196.7 10.6 %all-reduce.7 = (f32[]{:T(128)}, f32[]{:T(128)}) all-reduce(f32[]{:T(128)} %get-tuple-element.7, f32[]{:T(128)} %get-tuple-element.8), channel_id=1, replica_groups=mesh['mem'=4,'lat_0'=4,'lat_1'=2,'lat_2'=4,'lat_3'=2] {'lat_3'}, use_global_device_ids=true, to_apply=%region_6.7 | all-reduce | flops 2 | bytes 16 | tf_op jit(solution)/shard_map/psum | solution.py:47
  208.7 0.8 multiply_reduce_fusion
  209.5 1.9 convolution_bitcast_fusion.1
  211.3 1.3 copy.81
  212.6 16.5 %all_to_all.128 = f32[2,512,128]{2,0,1:T(2,128)S(1)} all-to-all(f32[2,512,128]{2,0,1:T(2,128)S(1)} %copy.81), channel_id=1, replica_groups=mesh['mem'=4,'lat_0'=4,'lat_1'=2,'lat_2'=4,'lat_3'=2] {'lat_0','lat_1','..., dimensions={1} | all-to-all | bytes 1048576 | tf_op jit(solution)/shard_map/all_to_all | solution.py:65
  229.2 6.8 %fusion.28 = f32[2,8,1024]{2,1,0:T(8,128)S(1)} fusion(f32[8,2,8,1024]{3,2,1,0:T(8,128)S(1)} %copy-done.1, f32[8,2,8,8,128]{4,2,3,1,0:T(8,128)S(1)} %bitcast.216, f32[1024,8,128,1,1]{2,1,0,4,3:T(8,128)} %bitcast.202), kind=kOutput, calls=%fused_computation.29 | convolution fusion | flops 1610858496 | bytes 5308416 | tf_op jit(solution)/shard_map/fbrc,nbc->frn/dot_general | solution.py:95
  236.1 11.6 %all_to_all.131 = f32[4,2,8,256]{3,2,1,0:T(8,128)S(1)} all-to-all(f32[4,2,8,256]{3,2,1,0:T(8,128)S(1)} %copy.85), channel_id=1, replica_groups=mesh['mem'=4,'lat_0'=4,'lat_1'=2,'lat_2'=4,'lat_3'=2] {'mem'}, dimensions={0} | all-to-all | bytes 131072 | tf_op jit(solution)/shard_map/all_to_all | solution.py:24
  247.7 3.6 gather_fusion.1
  251.5 23.9 %scatter_fusion.2 = f32[8,512]{1,0:T(8,128)S(1)} fusion(f32[8,512]{1,0:T(8,128)S(1)} %broadcast.43, s32[512]{0:T(512)S(1)} %reshape.118, f32[512]{0:T(512)S(1)} %reshape.132), kind=kCustom, calls=%fused_computation.4 | custom fusion | flops 512 | bytes 10240 | tf_op jit(solution)/shard_map/scatter-add | solution.py:79
  275.4 9.3 %all_to_all.129 = f32[4,2,8,256]{3,2,1,0:T(8,128)S(1)} all-to-all(f32[4,2,8,256]{3,2,1,0:T(8,128)S(1)} %broadcast_in_dim.22), channel_id=1, replica_groups=mesh['mem'=4,'lat_0'=4,'lat_1'=2,'lat_2'=4,'lat_3'=2] {'mem'}, dimensions={0} | all-to-all | bytes 131072 | tf_op jit(solution)/shard_map/all_to_all | solution.py:36
  284.7 4.6 %fusion = f32[16,8,8,128]{3,1,2,0:T(8,128)S(1)} fusion(f32[16,8,1024,1]{2,1,3,0:T(8,128)S(1)} %bitcast.208, f32[1024,1024]{1,0:T(8,128)} %param.11), kind=kOutput, calls=%fused_computation.6 | convolution fusion | flops 1610612736 | bytes 5242880 | tf_op jit(solution)/shard_map/frn,nbc->fbrc/dot_general | solution.py:72
  289.3 19.5 %all_to_all.130 = f32[128,8,128]{2,1,0:T(8,128)S(1)} all-to-all(f32[128,8,128]{2,1,0:T(8,128)S(1)} %bitcast.209), channel_id=1, replica_groups=mesh['mem'=4,'lat_0'=4,'lat_1'=2,'lat_2'=4,'lat_3'=2] {'lat_0','lat_1','..., dimensions={0} | all-to-all | bytes 1048576 | tf_op jit(solution)/shard_map/all_to_all | solution.py:62
  308.8 1.7 fusion.36
  310.5 7.8 %all-reduce.4 = (f32[]{:T(128)}, f32[]{:T(128)}) all-reduce(f32[]{:T(128)} %get-tuple-element.25, f32[]{:T(128)} %fusion.36), channel_id=1, replica_groups=mesh['mem'=4,'lat_0'=4,'lat_1'=2,'lat_2'=4,'lat_3'=2] {'mem'}, use_global_device_ids=true, to_apply=%region_17.19 | all-reduce | flops 2 | bytes 16 | tf_op jit(solution)/shard_map/psum | solution.py:47
  318.3 7.4 %all-reduce.2 = (f32[]{:T(128)}, f32[]{:T(128)}) all-reduce(f32[]{:T(128)} %get-tuple-element.13, f32[]{:T(128)} %get-tuple-element.14), channel_id=1, replica_groups=mesh['mem'=4,'lat_0'=4,'lat_1'=2,'lat_2'=4,'lat_3'=2] {'lat_0'}, use_global_device_ids=true, to_apply=%region_18.20 | all-reduce | flops 2 | bytes 16 | tf_op jit(solution)/shard_map/psum | solution.py:47
  325.7 4.4 %all-reduce.8 = (f32[]{:T(128)}, f32[]{:T(128)}) all-reduce(f32[]{:T(128)} %get-tuple-element.9, f32[]{:T(128)} %get-tuple-element.10), channel_id=1, replica_groups=mesh['mem'=4,'lat_0'=4,'lat_1'=2,'lat_2'=4,'lat_3'=2] {'lat_1'}, use_global_device_ids=true, to_apply=%region_19.21 | all-reduce | flops 2 | bytes 16 | tf_op jit(solution)/shard_map/psum | solution.py:47
  330.1 7.1 %all-reduce = (f32[]{:T(128)}, f32[]{:T(128)}) all-reduce(f32[]{:T(128)} %get-tuple-element.21, f32[]{:T(128)} %get-tuple-element.22), channel_id=1, replica_groups=mesh['mem'=4,'lat_0'=4,'lat_1'=2,'lat_2'=4,'lat_3'=2] {'lat_2'}, use_global_device_ids=true, to_apply=%region_20.22 | all-reduce | flops 2 | bytes 16 | tf_op jit(solution)/shard_map/psum | solution.py:47
  337.2 10.4 %all-reduce.6 = (f32[]{:T(128)}, f32[]{:T(128)}) all-reduce(f32[]{:T(128)} %get-tuple-element.5, f32[]{:T(128)} %get-tuple-element.6), channel_id=1, replica_groups=mesh['mem'=4,'lat_0'=4,'lat_1'=2,'lat_2'=4,'lat_3'=2] {'lat_3'}, use_global_device_ids=true, to_apply=%region_21.23 | all-reduce | flops 2 | bytes 16 | tf_op jit(solution)/shard_map/psum | solution.py:47
  349.0 1.0 copy.90
  350.0 4.4 %all-to-all-start.10 = ((f32[2,512,128]{2,0,1:T(2,128)}), f32[2,512,128]{2,0,1:T(2,128)S(1)}, u32[]{:S(2)}, u32[]{:S(2)}) async-start(f32[2,512,128]{2,0,1:T(2,128)} %copy.90), calls=%async_computation.10 | async-start | bytes 1048576 | tf_op jit(solution)/shard_map/all_to_all | solution.py:65
  355.0 11.9 %all-to-all-done.10 = f32[2,512,128]{2,0,1:T(2,128)S(1)} async-done(((f32[2,512,128]{2,0,1:T(2,128)}), f32[2,512,128]{2,0,1:T(2,128)S(1)}, u32[]{:S(2)}, u32[]{:S(2)}) %all-to-all-start.10) | async-done | bytes 524320 | tf_op jit(solution)/shard_map/all_to_all | solution.py:65
  367.0 0.8 copy.92
  (42 shorter events, 1.7 us)
Async XLA Ops:
  0.6 68.5 %copy-start = (f32[512,512]{1,0:T(8,128)S(1)}, f32[512,512]{1,0:T(8,128)}, u32[]{:S(2)}) copy-start(f32[512,512]{1,0:T(8,128)} %param.10) | copy-start | bytes 3145732
  2.3 39.8 %copy-start.1 = (f32[8,2,8,1024]{3,2,1,0:T(8,128)S(1)}, f32[8,2,8,1024]{3,2,1,0:T(8,128)}, u32[]{:S(2)}) copy-start(f32[8,2,8,1024]{3,2,1,0:T(8,128)} %param.9) | copy-start | bytes 1572868
  72.2 17.1 %all-to-all-start.2 = ((f32[2,512,128]{2,0,1:T(2,128)}), f32[2,512,128]{2,0,1:T(2,128)S(1)}, u32[]{:S(2)}, u32[]{:S(2)}) async-start(f32[2,512,128]{2,0,1:T(2,128)} %copy.72), calls=%async_computation.2 | async-start | bytes 1048576 | tf_op jit(solution)/shard_map/all_to_all | solution.py:65
  96.3 14.5 %copy-start.2 = (f32[8,64]{1,0:T(8,128)S(1)}, f32[8,64]{1,0:T(8,128)}, u32[]{:S(2)}) copy-start(f32[8,64]{1,0:T(8,128)} %param.13) | copy-start | bytes 6148
  96.3 14.5 %copy-start.3 = (s32[8,64]{1,0:T(8,128)S(1)}, s32[8,64]{1,0:T(8,128)}, u32[]{:S(2)}) copy-start(s32[8,64]{1,0:T(8,128)} %param.14) | copy-start | bytes 6148
  97.0 10.1 %all-to-all-start.3 = ((f32[4,2,8,256]{3,2,1,0:T(8,128)}), f32[4,2,8,256]{3,2,1,0:T(8,128)S(1)}, u32[]{:S(2)}, u32[]{:S(2)}) async-start(f32[4,2,8,256]{3,2,1,0:T(8,128)} %copy.76), calls=%async_computation.3 | async-start | bytes 131072 | tf_op jit(solution)/shard_map/all_to_all | solution.py:24
  350.0 17.0 %all-to-all-start.10 = ((f32[2,512,128]{2,0,1:T(2,128)}), f32[2,512,128]{2,0,1:T(2,128)S(1)}, u32[]{:S(2)}, u32[]{:S(2)}) async-start(f32[2,512,128]{2,0,1:T(2,128)} %copy.90), calls=%async_computation.10 | async-start | bytes 1048576 | tf_op jit(solution)/shard_map/all_to_all | solution.py:65
where the time goes:
time: 369 us; the launch traced here: 368 us
  blocking collectives  198 us (54%)
  other arithmetic  74.9 us (20%)
  matrix products  35 us (9%)
  waiting for transfers between devices  26.1 us (7%)
  local copies, waits for them, and re-layouts  17.9 us (5%)
  starting transfers between devices  12.3 us (3%)
    psum x10, blocking collectives, by_axis(): shard = lax.psum(shard, axis)  74.3 us
    scatter-add x3, other arithmetic, spread(): jnp.zeros((rows, levels * quarter), jnp.float32).at[row_ids, local_cell]  71.8 us
    all_to_all x3, blocking collectives, to_strips(): return lax.all_to_all(blocked, LAT, split_axis=0, concat_axis=1, tiled=True)  61.3 us
    all_to_all x3, blocking collectives, from_everyone(): lax.all_to_all(jnp.broadcast_to(shard[None], (count, *shard.shape)), axis...  34.4 us
    all_to_all x2, waiting for transfers between devices, to_rows(): return lax.all_to_all(strips, LAT, split_axis=1, concat_axis=0, tiled=True)  19.3 us
    all_to_all x1, blocking collectives, to_rows(): return lax.all_to_all(strips, LAT, split_axis=1, concat_axis=0, tiled=True)  16.5 us
    dot_general x3, matrix products, lon_adjoint(): blocked = jnp.einsum('frn,nbc->fbrc', field, lon_pair, precision=HIGH)  13.8 us
    dot_general x2, matrix products, per_device(): jnp.einsum('fbrc,nbc->frn', lon_shaped, lon_pair, precision=HIGH)  13.7 us
  transfers between devices with their start and end apart: 3, of which 3 were waited for; matrix products, arithmetic and copies ran while one was open for 2% of the time, Pallas kernels for 0%

commit v1 on v0

v1 whole, which is shorter than its diff:
```python
import jax
import jax.numpy as jnp
from jax import lax
from jax.sharding import Mesh
from jax.sharding import PartitionSpec as P

LAT = ("lat_0", "lat_1", "lat_2", "lat_3")
MEM_LAT = ("mem", "lat_0", "lat_1", "lat_2", "lat_3")
HIGH = lax.Precision.HIGH


def per_device(members, lat_root, lon_root, innovation, obs_weight, obs_mask, obs_cell):
    mem_dev, levels, rows, nlon = members.shape
    fields = mem_dev * levels
    parts = lax.axis_size("mem")
    quarter = nlon // parts
    nlat = lat_root.shape[0]
    strips = nlat // rows
    per_field = strips // fields
    width = nlon // per_field
    weights = obs_weight * obs_mask.astype(jnp.float32)
    local_cell = obs_cell // nlon * quarter + obs_cell % quarter
    hit = local_cell[:, :, None] == jnp.arange(levels * quarter, dtype=jnp.int32)

    def on_grid(values):
        flat = jnp.sum(jnp.where(hit, values[:, :, None], 0.0), axis=1)
        return flat.reshape(rows, levels, quarter).transpose(1, 0, 2)

    def whole_rows(field):
        return lax.all_gather(field, "mem", axis=2, tiled=True)

    def to_strips(field):
        blocks = field.reshape(fields, rows, per_field, width).transpose(0, 2, 1, 3)
        blocks = blocks.reshape(strips, rows, width)
        out = lax.all_to_all(blocks, LAT, split_axis=0, concat_axis=0, tiled=True)
        return out.reshape(nlat, width)

    def to_rows(strip):
        out = lax.all_to_all(strip.reshape(strips, rows, width), LAT, split_axis=0, concat_axis=0, tiled=True)
        return out.reshape(fields, per_field, rows, width).transpose(0, 2, 1, 3).reshape(fields * rows, nlon)

    def gradient_of(field):
        member_field = (members * whole_rows(field)[None]).reshape(fields * rows, nlon)
        return jnp.dot(lat_root.T, to_strips(jnp.dot(member_field, lon_root, precision=HIGH)), precision=HIGH)

    def image_of(gradient):
        mixed = to_rows(jnp.dot(lat_root, gradient, precision=HIGH))
        value = jnp.dot(mixed, lon_root.T, precision=HIGH).reshape(members.shape)
        return lax.psum_scatter(jnp.sum(members * value, axis=0), "mem", scatter_dimension=2, tiled=True)

    weight_field = on_grid(weights)
    gradient0 = gradient_of(on_grid(-(weights * innovation)))
    image0 = image_of(gradient0)
    seen0 = weight_field * image0
    sums0 = lax.psum(jnp.stack([jnp.sum(gradient0 * gradient0), jnp.sum(seen0 * image0)]), MEM_LAT)
    gradient_z = gradient_of(seen0)
    image_z = image_of(gradient_z)
    length0 = sums0[0] / (sums0[0] + sums0[1])
    keep = 1.0 - length0
    gradient1 = keep * gradient0 - length0 * gradient_z
    image1 = keep * image0 - length0 * image_z
    sums1 = lax.psum(
        jnp.stack([jnp.sum(gradient1 * gradient1), jnp.sum(weight_field * image1 * image1)]), MEM_LAT
    )
    length1 = sums1[0] / (sums1[0] + sums1[1])
    control = to_rows(-(length0 * gradient0) - length1 * gradient1)
    increment = -(length0 * image0) - length1 * image1
    return increment, control.reshape(members.shape)


def solution(mesh):
    finer = Mesh(
        mesh.devices.reshape(mesh.shape["mem"], 4, 2, 4, 2),
        ("mem", "lat_0", "lat_1", "lat_2", "lat_3"),
    )
    placed = (P("mem", None, LAT, None), P(), P(), P(LAT, "mem"), P(LAT, "mem"), P(LAT, "mem"), P(LAT, "mem"))
    return jax.shard_map(
        per_device,
        mesh=finer,
        in_specs=placed,
        out_specs=(P(None, LAT, "mem"), P("mem", None, LAT, None)),
        check_vma=False,
    )
```

time: 369 us -> 368 us (level)
  other arithmetic: 74.9 us -> 8.8 us
  blocking collectives: 198 us -> 237 us
  waiting for transfers between devices: 26.1 us -> 48.9 us
  between operations: 3.61 us -> 18.1 us
  matrix products: 35 us -> 24.3 us
  local copies, waits for them, and re-layouts: 17.9 us -> 9.83 us
  starting transfers between devices: 12.3 us -> 19.3 us
    psum x10 -> x2, blocking collectives: 74.3 us -> 154 us  [the longest x1 77.3 us: per_device(): lax.psum(jnp.stack([jnp.sum(gradient0 * gradient0), jnp.sum(seen0 * image...]
    scatter-add x3 -> x0, other arithmetic: 71.8 us -> none  [spread(): jnp.zeros((rows, levels * quarter), jnp.float32).at[row_ids, local_cell]]
    all_to_all x8 -> x3, blocking collectives: 124 us -> 57.4 us  [the longest x2 33.8 us: to_rows(): lax.all_to_all(strip.reshape(strips, rows, width), LAT, split_axis=0, con...]
    reduce_scatter x0 -> x2, waiting for transfers between devices: none -> 37.8 us  [image_of(): lax.psum_scatter(jnp.sum(members * value, axis=0), 'mem', scatter_dimensi...]
    all_gather x0 -> x2, blocking collectives: none -> 26.1 us  [whole_rows(): return lax.all_gather(field, 'mem', axis=2, tiled=True)]
    all_to_all x3 -> x2, waiting for transfers between devices: 26.1 us -> 11.1 us  [the longest x1 11.1 us: to_rows(): lax.all_to_all(strip.reshape(strips, rows, width), LAT, split_axis=0, con...]
    dot_general x10 -> x8, matrix products: 35 us -> 24.3 us  [the longest x2 10.1 us: image_of(): value = jnp.dot(mixed, lon_root.T, precision=HIGH).reshape(members.shape)]
    gather x5 -> x0, local copies, waits for them, and re-layouts: 7.41 us -> none  [per_device(): jnp.take_along_axis(observe_flat, local_cell, axis=1)]
  transfers between devices with their start and end apart: 3 -> 4, of which waited for: 3 -> 3; matrix products, arithmetic and copies ran while one was open for 2% -> 1% of each run, Pallas kernels for 0% -> 0%
where the time goes in v1:
time: 368 us; the launch traced here: 367 us
  blocking collectives  237 us (64%)
  waiting for transfers between devices  48.9 us (13%)
  matrix products  24.3 us (7%)
  starting transfers between devices  19.3 us (5%)
  between operations  18.1 us (5%)
  local copies, waits for them, and re-layouts  9.83 us (3%)
  other arithmetic  8.8 us (2%)
    psum x1, blocking collectives, per_device(): lax.psum(jnp.stack([jnp.sum(gradient0 * gradient0), jnp.sum(seen0 * image...  77.3 us
    psum x1, blocking collectives, per_device(): lax.psum(jnp.stack([jnp.sum(gradient1 * gradient1), jnp.sum(weight_field...  76.5 us
    reduce_scatter x2, waiting for transfers between devices, image_of(): lax.psum_scatter(jnp.sum(members * value, axis=0), 'mem', scatter_dimensi...  37.8 us
    all_to_all x2, blocking collectives, to_rows(): lax.all_to_all(strip.reshape(strips, rows, width), LAT, split_axis=0, con...  33.8 us
    all_gather x2, blocking collectives, whole_rows(): return lax.all_gather(field, 'mem', axis=2, tiled=True)  26.1 us
    all_to_all x1, blocking collectives, to_strips(): out = lax.all_to_all(blocks, LAT, split_axis=0, concat_axis=0, tiled=True)  23.6 us
    all_to_all x1, starting transfers between devices, to_strips(): out = lax.all_to_all(blocks, LAT, split_axis=0, concat_axis=0, tiled=True)  13.1 us
    all_to_all x1, waiting for transfers between devices, to_rows(): lax.all_to_all(strip.reshape(strips, rows, width), LAT, split_axis=0, con...  11.1 us
  transfers between devices with their start and end apart: 4, of which 3 were waited for; matrix products, arithmetic and copies ran while one was open for 1% of the time, Pallas kernels for 0%

profile of v1, /device:TPU:1, one launch (start us, length us, event | category | flops | bytes accessed | tf_op | source)
XLA Modules:
  0.0 366.7 jit_solution(12220235037679513709)
XLA Ops:
  7.2 0.0 copy-start
  7.2 0.0 reduce-scatter.3.cloned.1.call-start
  7.2 0.8 fusion.23
  8.0 0.7 multiply_negate_fusion
  8.7 0.4 select_reduce_fusion
  9.1 15.4 %all_gather.6 = f32[2,8,1024]{2,1,0:T(8,128)S(1)} all-gather(f32[2,8,256]{2,1,0:T(8,128)S(1)} %bitcast.109), channel_id=1, replica_groups=mesh['mem'=4,'lat_0'=4,'lat_1'=2,'lat_2'=4,'lat_3'=2] {'mem'}, dimensions={2}, use_global_device_ids=true | all-gather | bytes 81920 | tf_op jit(solution)/shard_map/all_gather | solution.py:30
  24.5 0.0 copy-start.1
  24.5 5.4 %copy.27 = f32[1024,1024]{1,0:T(8,128)} copy(f32[1024,1024]{0,1:T(8,128)} %bitcast.98) | data formatting | bytes 8388608 | tf_op jit(solution)/shard_map/dot_general | solution.py:44
  29.9 0.0 copy-done.1
  30.0 4.4 %fusion.28 = f32[16,8,4,256]{3,1,2,0:T(8,128)S(1)} fusion(f32[16,8,1024,1]{2,1,3,0:T(8,128)S(1)} %bitcast.100, f32[4,256,1024,1]{2,1,0,3:T(8,128)} %bitcast.96), kind=kOutput, calls=%fused_computation.46 | convolution fusion | flops 805306368 | bytes 5242880 | tf_op jit(solution)/shard_map/dot_general | solution.py:44
  34.4 23.6 %all_to_all.25 = f32[64,8,256]{2,1,0:T(8,128)S(1)} all-to-all(f32[64,8,256]{2,1,0:T(8,128)S(1)} %bitcast.101), channel_id=1, replica_groups=mesh['mem'=4,'lat_0'=4,'lat_1'=2,'lat_2'=4,'lat_3'=2] {'lat_0','lat_1','..., dimensions={0} | all-to-all | bytes 1048576 | tf_op jit(solution)/shard_map/all_to_all | solution.py:35
  58.0 0.0 copy-done
  58.0 1.3 multiply_reduce_fusion.1
  59.3 0.6 convolution_bitcast_fusion.1
  59.9 0.2 copy.20
  60.1 16.9 %all_to_all.26 = f32[64,8,256]{2,1,0:T(8,128)S(1)} all-to-all(f32[64,8,256]{2,1,0:T(8,128)S(1)} %bitcast.103), channel_id=1, replica_groups=mesh['mem'=4,'lat_0'=4,'lat_1'=2,'lat_2'=4,'lat_3'=2] {'lat_0','lat_1','..., dimensions={0} | all-to-all | bytes 1048576 | tf_op jit(solution)/shard_map/all_to_all | solution.py:39
  77.0 5.0 %fusion.13 = f32[2,8,1024]{2,1,0:T(8,128)} fusion(f32[8,2,8,1024]{3,2,1,0:T(8,128)S(1)} %copy-done.1, f32[8,2,8,1024]{3,2,1,0:T(8,128)S(1)} %bitcast.105, f32[1024,1024]{1,0:T(8,128)} %param.9), kind=kOutput, calls=%fused_computation.9 | convolution fusion | flops 805552128 | bytes 5308416 | tf_op jit(solution)/shard_map/dot_general | solution.py:48
  82.0 0.0 reduce-scatter.3.cloned.1.call-update
  82.0 18.9 %reduce-scatter.3.cloned.1.call-done = f32[2,8,256]{2,1,0:T(8,128)} async-done(((f32[2,8,1024]{2,1,0:T(8,128)}), f32[2,8,256]{2,1,0:T(8,128)}) %reduce-scatter.3.cloned.1.call-update) | async-done | bytes 16400 | tf_op jit(solution)/shard_map/reduce_scatter | solution.py:49
  101.0 1.4 multiply_reduce_fusion.2
  102.3 10.8 %all_gather.7 = f32[2,8,1024]{2,1,0:T(8,128)S(1)} all-gather(f32[2,8,256]{2,1,0:T(8,128)S(1)} %get-tuple-element.5), channel_id=1, replica_groups=mesh['mem'=4,'lat_0'=4,'lat_1'=2,'lat_2'=4,'lat_3'=2] {'mem'}, dimensions={2}, use_global_device_ids=true | all-gather | bytes 81920 | tf_op jit(solution)/shard_map/all_gather | solution.py:30
  113.1 5.2 %fusion.29 = f32[16,8,4,256]{3,1,2,0:T(8,128)} fusion(f32[16,8,1024,1]{2,1,3,0:T(8,128)S(1)} %bitcast.99, f32[4,256,1024,1]{2,1,0,3:T(8,128)} %bitcast.97), kind=kOutput, calls=%fused_computation.47 | convolution fusion | flops 805306368 | bytes 5242880 | tf_op jit(solution)/shard_map/dot_general | solution.py:44
  118.3 13.1 %all-to-all-start.2 = ((f32[64,8,256]{2,1,0:T(8,128)}), f32[64,8,256]{2,1,0:T(8,128)S(1)}, u32[]{:S(2)}, u32[]{:S(2)}) async-start(f32[64,8,256]{2,1,0:T(8,128)} %bitcast.28), calls=%async_computation.3 | async-start | bytes 1048576 | tf_op jit(solution)/shard_map/all_to_all | solution.py:35
  131.5 0.0 reduce-scatter.5.cloned.1.call-start
  131.5 1.3 pad_maximum_fusion
  132.8 77.3 %psum.14 = f32[2]{0:T(128)S(1)} all-reduce(f32[2]{0:T(128)S(1)} %pad_maximum_fusion), channel_id=1, replica_groups=mesh['mem'=4,'lat_0'=4,'lat_1'=2,'lat_2'=4,'lat_3'=2] {'mem','lat_0','la..., use_global_device_ids=true, to_apply=%region_6.7 | all-reduce | flops 2 | bytes 16 | tf_op jit(solution)/shard_map/psum | solution.py:55
  210.1 0.6 fusion.27
  212.7 0.0 all-to-all-done.2
  212.7 1.3 multiply_reduce_fusion
  214.0 1.4 convolution_bitcast_fusion
  215.5 1.2 copy.22
  216.7 16.9 %all_to_all.27 = f32[64,8,256]{2,1,0:T(8,128)S(1)} all-to-all(f32[64,8,256]{2,1,0:T(8,128)S(1)} %bitcast.104), channel_id=1, replica_groups=mesh['mem'=4,'lat_0'=4,'lat_1'=2,'lat_2'=4,'lat_3'=2] {'lat_0','lat_1','..., dimensions={0} | all-to-all | bytes 1048576 | tf_op jit(solution)/shard_map/all_to_all | solution.py:39
  233.6 0.0 copy-start.2
  233.6 5.1 %fusion.10 = f32[2,8,1024]{2,1,0:T(8,128)} fusion(f32[8,2,8,1024]{3,2,1,0:T(8,128)S(1)} %copy-done.1, f32[8,2,8,1024]{3,2,1,0:T(8,128)S(1)} %bitcast.106, f32[1024,1024]{1,0:T(8,128)} %param.9), kind=kOutput, calls=%fused_computation.8 | convolution fusion | flops 805552128 | bytes 5308416 | tf_op jit(solution)/shard_map/dot_general | solution.py:48
  238.7 0.0 reduce-scatter.5.cloned.1.call-update
  238.7 18.9 %reduce-scatter.5.cloned.1.call-done = f32[2,8,256]{2,1,0:T(8,128)} async-done(((f32[2,8,1024]{2,1,0:T(8,128)}), f32[2,8,256]{2,1,0:T(8,128)}) %reduce-scatter.5.cloned.1.call-update) | async-done | bytes 16400 | tf_op jit(solution)/shard_map/reduce_scatter | solution.py:49
  257.6 0.0 copy-done.2
  257.6 1.3 fusion.20
  258.9 1.4 pad_maximum_fusion.1
  260.3 76.5 %psum.15 = f32[2]{0:T(128)S(1)} all-reduce(f32[2]{0:T(128)S(1)} %pad_maximum_fusion.1), channel_id=1, replica_groups=mesh['mem'=4,'lat_0'=4,'lat_1'=2,'lat_2'=4,'lat_3'=2] {'mem','lat_0','la..., use_global_device_ids=true, to_apply=%region_11.12 | all-reduce | flops 2 | bytes 16 | tf_op jit(solution)/shard_map/psum | solution.py:62
  336.8 0.6 fusion.26
  339.3 0.1 subtract_bitcast_fusion
  339.4 1.0 copy.23
  340.4 6.1 %all-to-all-start.4 = ((f32[64,8,256]{2,1,0:T(8,128)}), f32[64,8,256]{2,1,0:T(8,128)S(1)}, u32[]{:S(2)}, u32[]{:S(2)}) async-start(f32[64,8,256]{2,1,0:T(8,128)} %bitcast.42), calls=%async_computation.6 | async-start | bytes 1048576 | tf_op jit(solution)/shard_map/all_to_all | solution.py:39
  346.6 1.3 multiply_subtract_fusion.1
  347.9 11.1 %all-to-all-done.4 = f32[64,8,256]{2,1,0:T(8,128)S(1)} async-done(((f32[64,8,256]{2,1,0:T(8,128)}), f32[64,8,256]{2,1,0:T(8,128)S(1)}, u32[]{:S(2)}, u32[]{:S(2)}) %all-to-all-start.4) | async-done | bytes 524320 | tf_op jit(solution)/shard_map/all_to_all | solution.py:39
  359.0 0.8 copy.29
  (2 shorter events, 0.1 us)
Async XLA Ops:
  7.2 50.8 %copy-start = (f32[512,512]{1,0:T(8,128)S(1)}, f32[512,512]{1,0:T(8,128)}, u32[]{:S(2)}) copy-start(f32[512,512]{1,0:T(8,128)} %param.8) | copy-start | bytes 3145732
  7.2 93.8 %reduce-scatter.3.cloned.1.call-start = ((), (), s32[]{:S(2)}) async-start(), calls=%async_computation.7 | async-start | bytes 81920 | tf_op jit(solution)/shard_map/reduce_scatter | solution.py:49
  24.5 5.4 %copy-start.1 = (f32[8,2,8,1024]{3,2,1,0:T(8,128)S(1)}, f32[8,2,8,1024]{3,2,1,0:T(8,128)}, u32[]{:S(2)}) copy-start(f32[8,2,8,1024]{3,2,1,0:T(8,128)} %param.7) | copy-start | bytes 1572868
  118.3 94.4 %all-to-all-start.2 = ((f32[64,8,256]{2,1,0:T(8,128)}), f32[64,8,256]{2,1,0:T(8,128)S(1)}, u32[]{:S(2)}, u32[]{:S(2)}) async-start(f32[64,8,256]{2,1,0:T(8,128)} %bitcast.28), calls=%async_computation.3 | async-start | bytes 1048576 | tf_op jit(solution)/shard_map/all_to_all | solution.py:35
  131.5 126.1 %reduce-scatter.5.cloned.1.call-start = ((), (), s32[]{:S(2)}) async-start(), calls=%async_computation.8 | async-start | bytes 81920 | tf_op jit(solution)/shard_map/reduce_scatter | solution.py:49
  233.6 24.0 %copy-start.2 = (f32[2,8,256]{2,1,0:T(8,128)S(1)}, f32[2,8,256]{2,1,0:T(8,128)}, u32[]{:S(2)}) copy-start(f32[2,8,256]{2,1,0:T(8,128)} %reduce-scatter.3.cloned.1.call-done) | copy-start | bytes 49156
  340.4 18.6 %all-to-all-start.4 = ((f32[64,8,256]{2,1,0:T(8,128)}), f32[64,8,256]{2,1,0:T(8,128)S(1)}, u32[]{:S(2)}, u32[]{:S(2)}) async-start(f32[64,8,256]{2,1,0:T(8,128)} %bitcast.42), calls=%async_computation.6 | async-start | bytes 1048576 | tf_op jit(solution)/shard_map/all_to_all | solution.py:39
Sparse Core Ops, SparseCore 0:
  82.2 18.7 reduce-scatter.2
  238.8 18.7 reduce-scatter.4

commit v2 on v1

v2 whole, which is shorter than its diff:
```python
import functools

import jax
import jax.numpy as jnp
from jax import lax
from jax.experimental import pallas as pl
from jax.experimental.pallas import tpu as pltpu
from jax.sharding import PartitionSpec as P

MESH = pl.DeviceIdType.MESH
F32 = jnp.float32
BF16 = jnp.bfloat16
NN = (((1,), (0,)), ((), ()))
NT = (((1,), (1,)), ((), ()))


def halves(x):
    high = x.astype(BF16)
    return high, (x - high.astype(F32)).astype(BF16)


def product(a, b, dims=NN):
    dot = functools.partial(lax.dot_general, dimension_numbers=dims, preferred_element_type=F32)
    return dot(a[0], b[0]) + (dot(a[0], b[1]) + dot(a[1], b[0]))


def kernel(
    members, a_hbm, b_hbm, innovation, obs_weight, obs_mask, obs_cell,
    increment, control,
    a_all, b_all, a_hi, a_lo, at_hi, at_lo, b_hi, b_lo, s_hi, s_lo,
    field, wfield, t_out, strip, grad, mixed, mixed_rows, grad_rows, value,
    part, got, image, sums, box_mem, box_a, box_b,
    load_sem, field_send, field_recv, t_send, t_recv, x_send, x_recv, g_send, g_recv,
    part_send, part_recv, mem_send, mem_recv, a_send, a_recv, b_send, b_recv,
):
    mem_dev, levels, rows, nlon = members.shape
    fields = mem_dev * levels
    parts = lax.axis_size("mem")
    strips = lax.axis_size("lat")
    per_field = strips // fields
    width = nlon // per_field
    nlat = strips * rows
    side = 8
    mem = lax.axis_index("mem")
    me = lax.axis_index("lat")
    my_field, my_part = me // per_field, me % per_field

    load_b = pltpu.make_async_copy(b_hbm, b_all, load_sem.at[0])
    load_a = pltpu.make_async_copy(a_hbm, a_all, load_sem.at[1])
    load_b.start()
    load_a.start()

    barrier = pltpu.get_barrier_semaphore()

    @pl.loop(1, strips)
    def _(k):
        pl.semaphore_signal(barrier, inc=1, device_id=(mem, (me + k) % strips), device_id_type=MESH)

    for k in range(1, parts):
        pl.semaphore_signal(barrier, inc=1, device_id=((mem + k) % parts, me), device_id_type=MESH)

    weights = obs_weight[...] * obs_mask[...].astype(F32)
    pulled = -(weights * innovation[...])
    cells = obs_cell[...]
    local = (cells // nlon) * width + cells % width
    spots = lax.broadcasted_iota(jnp.int32, (rows, levels * width), 1)
    wsum = jnp.zeros((rows, levels * width), F32)
    hsum = jnp.zeros((rows, levels * width), F32)
    for j in range(cells.shape[1]):
        hit = local[:, j : j + 1] == spots
        wsum = wsum + jnp.where(hit, weights[:, j : j + 1], 0.0)
        hsum = hsum + jnp.where(hit, pulled[:, j : j + 1], 0.0)
    for l in range(levels):
        wfield[l] = wsum[:, l * width : (l + 1) * width]
        field[0, mem, l] = hsum[:, l * width : (l + 1) * width]

    pl.semaphore_wait(barrier, strips - 1 + parts - 1)

    def bytes_of(ref, sem):
        return pltpu.make_async_copy(ref, ref, sem)

    def share_field(b):
        for k in range(1, parts):
            pltpu.make_async_remote_copy(
                src_ref=field.at[b, mem],
                dst_ref=field.at[b, mem],
                send_sem=field_send.at[b],
                recv_sem=field_recv.at[b],
                device_id=((mem + k) % parts, me),
                device_id_type=MESH,
            ).start()

    share_field(0)
    load_b.wait()
    for q in range(per_field):
        high, low = halves(b_all[:, q * width : (q + 1) * width])
        b_hi[q] = high
        b_lo[q] = low
    load_a.wait()
    high, low = halves(a_all[...])
    a_hi[...] = high
    a_lo[...] = low
    high, low = halves(a_all[...].T)
    at_hi[...] = high
    at_lo[...] = low

    def gradient_of(b):
        bytes_of(field.at[b, pl.ds(0, parts - 1)], field_recv.at[b]).wait()
        for q in range(per_field):
            high, low = halves(
                (members[:, :, :, q * width : (q + 1) * width] * field[b, q][None]).reshape(fields * rows, width)
            )
            s_hi[:, q * width : (q + 1) * width] = high
            s_lo[:, q * width : (q + 1) * width] = low

        @pl.loop(0, per_field)
        def _(t):
            q = (my_part + t) % per_field
            t_out[b, q] = product((s_hi[...], s_lo[...]), (b_hi[q], b_lo[q]))

            @pl.loop(0, fields)
            def _(k):
                f = (my_field + k) % fields
                d = f * per_field + q

                @pl.when(d != me)
                def _():
                    pltpu.make_async_remote_copy(
                        src_ref=t_out.at[b, q, pl.ds(f * rows, rows)],
                        dst_ref=strip.at[b, pl.ds(me * rows, rows)],
                        send_sem=t_send.at[b],
                        recv_sem=t_recv.at[b],
                        device_id=(mem, d),
                        device_id_type=MESH,
                    ).start()

                @pl.when(d == me)
                def _():
                    pltpu.make_async_copy(
                        t_out.at[b, q, pl.ds(f * rows, rows)], strip.at[b, pl.ds(me * rows, rows)], t_recv.at[b]
                    ).start()

        bytes_of(strip.at[b], t_recv.at[b]).wait()
        grad[b] = product((at_hi[...], at_lo[...]), halves(strip[b]))

    def to_rows(b, source, target, send, recv):
        @pl.loop(1, strips)
        def _(k):
            d = (me + k) % strips
            pltpu.make_async_remote_copy(
                src_ref=source.at[b, pl.ds(d * rows, rows)],
                dst_ref=target.at[b, my_part, pl.ds(my_field * rows, rows)],
                send_sem=send.at[b],
                recv_sem=recv.at[b, my_part],
                device_id=(mem, d),
                device_id_type=MESH,
            ).start()

        pltpu.make_async_copy(
            source.at[b, pl.ds(me * rows, rows)],
            target.at[b, my_part, pl.ds(my_field * rows, rows)],
            recv.at[b, my_part],
        ).start()

    def image_of(b):
        mixed[b] = product((a_hi[...], a_lo[...]), halves(grad[b]))
        to_rows(b, mixed, mixed_rows, x_send, x_recv)
        to_rows(b, grad, grad_rows, g_send, g_recv)
        for q in range(per_field):
            bytes_of(mixed_rows.at[b, q], x_recv.at[b, q]).wait()
            term = product(halves(mixed_rows[b, q]), (b_hi[q], b_lo[q]), NT)
            value[...] = term if q == 0 else value[...] + term
        for q in range(parts):
            shaped = value[:, q * width : (q + 1) * width].reshape(mem_dev, levels, rows, width)
            part[b, q] = jnp.sum(members[:, :, :, q * width : (q + 1) * width] * shaped, axis=0)
        for k in range(1, parts):
            other = (mem + k) % parts
            pltpu.make_async_remote_copy(
                src_ref=part.at[b, other],
                dst_ref=got.at[b, mem],
                send_sem=part_send.at[b],
                recv_sem=part_recv.at[b],
                device_id=(other, me),
                device_id_type=MESH,
            ).start()
        got[b, mem] = part[b, mem]
        bytes_of(got.at[b, pl.ds(0, parts - 1)], part_recv.at[b]).wait()
        image[b] = jnp.sum(got[b], axis=0)

    def lanes(x):
        return jnp.sum(x.reshape(-1, 8, 128), axis=0).sum(axis=0, keepdims=True)

    def start_round(b, box, slot, device, count, send, recv):
        @pl.loop(1, count)
        def _(k):
            pltpu.make_async_remote_copy(
                src_ref=sums.at[b],
                dst_ref=box.at[b, slot],
                send_sem=send.at[b],
                recv_sem=recv.at[b],
                device_id=device((slot + k) % count),
                device_id_type=MESH,
            ).start()

        box[b, slot] = sums[b]

    def end_round(b, box, count, send, recv):
        bytes_of(box.at[b, pl.ds(0, count - 1)], recv.at[b]).wait()
        bytes_of(box.at[b, pl.ds(0, count - 1)], send.at[b]).wait()
        sums[b] = jnp.sum(box[b], axis=0)

    def all_sums(b, norm, seen):
        row = lax.broadcasted_iota(jnp.int32, (8, 128), 0)
        sums[b] = jnp.where(row == 0, lanes(norm), 0.0) + jnp.where(row == 1, lanes(seen), 0.0)
        hi, lo = me // side, me % side
        start_round(b, box_mem, mem, lambda k: (k, me), parts, mem_send, mem_recv)
        end_round(b, box_mem, parts, mem_send, mem_recv)
        start_round(b, box_a, hi, lambda k: (mem, k * side + lo), side, a_send, a_recv)
        end_round(b, box_a, side, a_send, a_recv)
        start_round(b, box_b, lo, lambda k: (mem, hi * side + k), side, b_send, b_recv)
        end_round(b, box_b, side, b_send, b_recv)
        total = sums[b]
        norm = jnp.sum(total[0:1])
        return norm / (norm + jnp.sum(total[1:2]))

    def squares(x, w=None):
        y = x * x if w is None else x * x * w
        return (y[:, :128] + y[:, 128:]).reshape(-1, 8, 128)

    gradient_of(0)
    image_of(0)
    image0 = image[0]
    for l in range(levels):
        field[1, mem, l] = wfield[l] * image0[l]
    share_field(1)
    seen = squares(image0.reshape(levels * rows, width), wfield[...].reshape(levels * rows, width))
    norm0 = squares(grad[0])
    length0 = all_sums(0, norm0, seen)
    gradient_of(1)
    image_of(1)
    keep = 1.0 - length0
    image1 = keep * image0 - length0 * image[1]
    seen = squares(image1.reshape(levels * rows, width), wfield[...].reshape(levels * rows, width))
    norm1 = squares(keep * grad[0] - length0 * grad[1])
    length1 = all_sums(1, norm1, seen)
    first = -(length0 + length1 * keep)
    second = length1 * length0
    increment[...] = first * image0 + second * image[1]
    for b in range(2):
        for q in range(per_field):
            bytes_of(grad_rows.at[b, q], g_recv.at[b, q]).wait()
    for q in range(per_field):
        block = first * grad_rows[0, q] + second * grad_rows[1, q]
        control[:, :, :, q * width : (q + 1) * width] = block.reshape(mem_dev, levels, rows, width)
    for b in range(2):
        sent = strip.at[b, pl.ds(0, nlat - rows)]
        bytes_of(sent, t_send.at[b]).wait()
        bytes_of(sent, x_send.at[b]).wait()
        bytes_of(sent, g_send.at[b]).wait()
        bytes_of(field.at[b, pl.ds(0, parts - 1)], field_send.at[b]).wait()
        bytes_of(field.at[b, pl.ds(0, parts - 1)], part_send.at[b]).wait()


def solution(mesh):
    parts, strips = mesh.shape["mem"], mesh.shape["lat"]

    def per_device(members, lat_root, lon_root, innovation, obs_weight, obs_mask, obs_cell):
        mem_dev, levels, rows, nlon = members.shape
        nlat = lat_root.shape[0]
        fields = mem_dev * levels
        per_field = strips // fields
        width = nlon // per_field
        lines = fields * rows
        vmem = pl.BlockSpec(memory_space=pltpu.VMEM)
        whole = pl.BlockSpec(memory_space=pl.ANY)
        pair = pltpu.SemaphoreType.DMA((2,))
        quads = pltpu.SemaphoreType.DMA((2, per_field))
        scratch = [
            pltpu.VMEM((nlat, nlat), F32),
            pltpu.VMEM((nlon, nlon), F32),
            *[pltpu.VMEM((nlat, nlat), BF16)] * 4,
            *[pltpu.VMEM((per_field, nlon, width), BF16)] * 2,
            *[pltpu.VMEM((lines, nlon), BF16)] * 2,
            pltpu.VMEM((2, parts, levels, rows, width), F32),
            pltpu.VMEM((levels, rows, width), F32),
            pltpu.VMEM((2, per_field, lines, width), F32),
            *[pltpu.VMEM((2, nlat, width), F32)] * 3,
            *[pltpu.VMEM((2, per_field, lines, width), F32)] * 2,
            pltpu.VMEM((lines, nlon), F32),
            *[pltpu.VMEM((2, parts, levels, rows, width), F32)] * 2,
            pltpu.VMEM((2, levels, rows, width), F32),
            pltpu.VMEM((2, 8, 128), F32),
            pltpu.VMEM((2, parts, 8, 128), F32),
            pltpu.VMEM((2, 8, 8, 128), F32),
            pltpu.VMEM((2, 8, 8, 128), F32),
            pair,
            pair, pair, pair, pair,
            pair, quads, pair, quads,
            *[pair] * 8,
        ]
        return pl.pallas_call(
            kernel,
            out_shape=(
                jax.ShapeDtypeStruct((levels, rows, nlon // parts), F32),
                jax.ShapeDtypeStruct(members.shape, F32),
            ),
            in_specs=[vmem, whole, whole, vmem, vmem, vmem, vmem],
            out_specs=(vmem, vmem),
            scratch_shapes=scratch,
            compiler_params=pltpu.CompilerParams(
                collective_id=0, has_side_effects=True, vmem_limit_bytes=48 * 1024 * 1024
            ),
            cost_estimate=pl.CostEstimate(flops=5_000_000_000, bytes_accessed=7_000_000, transcendentals=0),
        )(members, lat_root, lon_root, innovation, obs_weight, obs_mask, obs_cell)

    return jax.shard_map(
        per_device,
        mesh=mesh,
        in_specs=(P("mem", None, "lat", None), P(), P(), *[P("lat", "mem")] * 4),
        out_specs=(P(None, "lat", "mem"), P("mem", None, "lat", None)),
        check_vma=False,
    )
```

time: 368 us -> 109 us (0.30)
  blocking collectives: 237 us -> 0 us
  Pallas kernels: 0 us -> 101 us
  waiting for transfers between devices: 48.9 us -> 0 us
  matrix products: 24.3 us -> 0 us
  starting transfers between devices: 19.3 us -> 0 us
  between operations: 18.1 us -> 0.65 us
  other arithmetic: 8.8 us -> 0 us
    psum x2 -> x0, blocking collectives: 154 us -> none  [the longest x1 77.3 us: per_device(): lax.psum(jnp.stack([jnp.sum(gradient0 * gradient0), jnp.sum(seen0 * image...]
    pallas_call x0 -> x1, Pallas kernels: none -> 101 us  [per_device(): pl.pallas_call(kernel, out_shape=(jax.ShapeDtypeStruct((levels, rows, nlo...]
    all_to_all x3 -> x0, blocking collectives: 57.4 us -> none  [the longest x2 33.8 us: to_rows(): lax.all_to_all(strip.reshape(strips, rows, width), LAT, split_axis=0, con...]
    reduce_scatter x2 -> x0, waiting for transfers between devices: 37.8 us -> none  [image_of(): lax.psum_scatter(jnp.sum(members * value, axis=0), 'mem', scatter_dimensi...]
    all_gather x2 -> x0, blocking collectives: 26.1 us -> none  [whole_rows(): return lax.all_gather(field, 'mem', axis=2, tiled=True)]
    dot_general x8 -> x0, matrix products: 24.3 us -> none  [the longest x2 10.1 us: image_of(): value = jnp.dot(mixed, lon_root.T, precision=HIGH).reshape(members.shape)]
    all_to_all x2 -> x0, starting transfers between devices: 19.3 us -> none  [the longest x1 13.1 us: to_strips(): out = lax.all_to_all(blocks, LAT, split_axis=0, concat_axis=0, tiled=True)]
    all_to_all x2 -> x0, waiting for transfers between devices: 11.1 us -> none  [the longest x1 11.1 us: to_rows(): lax.all_to_all(strip.reshape(strips, rows, width), LAT, split_axis=0, con...]
  transfers between devices with their start and end apart: 4 -> 0, of which waited for: 3 -> 0; matrix products, arithmetic and copies ran while one was open for 1% -> 0% of each run, Pallas kernels for 0% -> 0%
where the time goes in v2:
time: 109 us; the launch traced here: 108 us
  Pallas kernels  101 us (93%)
  local copies, waits for them, and re-layouts  6.4 us (6%)
    pallas_call x1, Pallas kernels, per_device(): pl.pallas_call(kernel, out_shape=(jax.ShapeDtypeStruct((levels, rows, nlo...  101 us
    unnamed x14, local copies, waits for them, and re-layouts  6.4 us

profile of v2, /device:TPU:1, one launch (start us, length us, event | category | flops | bytes accessed | tf_op | source)
XLA Modules:
  0.0 108.3 jit_solution(8900173293100390411)
XLA Ops:
  0.6 0.0 copy-start
  0.6 1.2 %copy-done = f32[512,512]{1,0:T(8,128)S(1)} copy-done((f32[512,512]{1,0:T(8,128)S(1)}, f32[512,512]{1,0:T(8,128)}, u32[]{:S(2)}) %copy-start) | copy-done | bytes 1048600
  1.9 0.0 copy-start.1
  1.9 1.0 copy-done.1
  2.9 0.0 copy-start.2
  2.9 0.7 copy-done.2
  3.6 0.0 copy-start.3
  3.6 0.7 copy-done.3
  4.3 0.0 copy-start.4
  4.3 0.7 copy-done.4
  5.0 0.0 copy-start.5
  5.0 0.7 copy-done.5
  5.6 101.3 %shard_map.86 = (f32[2,8,256]{2,1,0:T(8,128)S(1)}, f32[8,2,8,1024]{3,2,1,0:T(8,128)S(1)}) custom-call(f32[8,2,8,1024]{3,2,1,0:T(8,128)S(1)} %copy-done.1, f32[512,512]{1,0:T(8,128)S(1)} %copy-done, f32[1024,1024]{1,0:T(8,128)} %b_hbm.1, f32[8,64]{1,0:T(8,128)S(1)} %copy-done.2, f32[8,64]{1,0:T(8,128)S(1)} %copy-done.3, s32[8,64]{1,0:T(8,128)S(1)} %copy-done.4, ...), custom_call_target="tpu_custom_call" | custom-call | flops 5000000000 | bytes 7000000 | tf_op jit(solution)/shard_map/pallas_call | solution.py:301
  106.9 0.6 copy.11
  107.5 0.8 copy.12
Async XLA Ops:
  0.6 1.2 %copy-start = (f32[512,512]{1,0:T(8,128)S(1)}, f32[512,512]{1,0:T(8,128)}, u32[]{:S(2)}) copy-start(f32[512,512]{1,0:T(8,128)} %a_hbm.1) | copy-start | bytes 3145732
  1.9 1.0 copy-start.1
  2.9 0.7 copy-start.2
  3.6 0.7 copy-start.3
  4.3 0.7 copy-start.4
  5.0 0.7 copy-start.5

commit v3 on v2

v3 whole, which is shorter than its diff:
```python
import functools

import jax
import jax.numpy as jnp
from jax import lax
from jax.experimental import pallas as pl
from jax.experimental.pallas import tpu as pltpu
from jax.sharding import PartitionSpec as P

MESH = pl.DeviceIdType.MESH
F32 = jnp.float32
BF16 = jnp.bfloat16
NN = (((1,), (0,)), ((), ()))
NT = (((1,), (1,)), ((), ()))


def halves(x):
    high = x.astype(BF16)
    return high, (x - high.astype(F32)).astype(BF16)


def product(a, b):
    dot = functools.partial(jnp.dot, preferred_element_type=F32)
    return dot(a[0], b[0]) + (dot(a[0], b[1]) + dot(a[1], b[0]))


def stacked_product(stack, b, dims):
    dot = functools.partial(lax.dot_general, dimension_numbers=dims, preferred_element_type=F32)
    lines = stack.shape[0] // 2
    both = dot(stack, b[0])
    return both[:lines] + (both[lines:] + dot(stack[:lines], b[1]))


def kernel(
    members_hbm, a_hbm, b_hbm, innovation_hbm, weight_hbm, mask_hbm, cell_hbm,
    increment, control,
    members, innovation, obs_weight, obs_mask, obs_cell, a_all, b_all, k_hi, k_lo, at_hi, at_lo, b_hi, b_lo, stack,
    field, wfield, t_out, strip, strip_hi, strip_lo, grad, mixed, mixed_rows, grad_rows, value,
    part, got, image, sums, box,
    load_sem, field_send, field_recv, t_send, t_recv, x_send, x_recv, g_send, g_recv,
    part_send, part_recv, box_send, box_recv,
):
    mem_dev, levels, rows, nlon = members.shape
    parts = lax.axis_size("mem")
    strips = lax.axis_size("lat")
    per_field = strips // (mem_dev * levels)
    width = nlon // per_field
    nlat = strips * rows
    lines = mem_dev * rows
    mem = lax.axis_index("mem")
    me = lax.axis_index("lat")

    side = 4
    x, z, y, core = me // 16, me // 8 % 2, me // 2 % 4, me % 2
    column = mem * side + z * 2 + core
    plane = x * side + y
    my_member, my_part = x * 2 + z, (x + y) % per_field

    def strip_device(m, l, q):
        return m // 2 * 16 + m % 2 * 8 + (q - m // 2 + per_field) % per_field * 2 + l

    def in_column(k):
        return k // side, x * 16 + k % side // 2 * 8 + y * 2 + k % 2

    def in_plane(k):
        return mem, k // side * 16 + z * 8 + k % side * 2 + core

    loads = [
        pltpu.make_async_copy(source, target, load_sem.at[k])
        for k, (source, target) in enumerate([
            (weight_hbm, obs_weight), (mask_hbm, obs_mask), (innovation_hbm, innovation), (cell_hbm, obs_cell),
            (b_hbm, b_all), (members_hbm, members), (a_hbm, a_all),
        ])
    ]
    for load in loads:
        load.start()

    barrier = pltpu.get_barrier_semaphore()

    @pl.loop(1, strips)
    def _(k):
        pl.semaphore_signal(barrier, inc=1, device_id=(mem, (me + k) % strips), device_id_type=MESH)

    @pl.loop(0, parts * side)
    def _(k):
        @pl.when(k // side != mem)
        def _():
            pl.semaphore_signal(barrier, inc=1, device_id=in_column(k), device_id_type=MESH)

    for load in loads[:4]:
        load.wait()
    weights = obs_weight[...] * obs_mask[...].astype(F32)
    pulled = -(weights * innovation[...])
    cells = obs_cell[...]
    local = (cells // nlon) * width + cells % width
    spots = lax.broadcasted_iota(jnp.int32, (rows, levels * width), 1)
    wsum = jnp.zeros((rows, levels * width), F32)
    hsum = jnp.zeros((rows, levels * width), F32)
    for j in range(cells.shape[1]):
        hit = local[:, j : j + 1] == spots
        wsum = wsum + jnp.where(hit, weights[:, j : j + 1], 0.0)
        hsum = hsum + jnp.where(hit, pulled[:, j : j + 1], 0.0)
    for l in range(levels):
        wfield[l] = wsum[:, l * width : (l + 1) * width]
        field[0, l, mem] = hsum[:, l * width : (l + 1) * width]

    pl.semaphore_wait(barrier, strips - 1 + (parts - 1) * side)

    def bytes_of(ref, sem):
        return pltpu.make_async_copy(ref, ref, sem)

    def share_field(b, l):
        for k in range(1, parts):
            pltpu.make_async_remote_copy(
                src_ref=field.at[b, l, mem],
                dst_ref=field.at[b, l, mem],
                send_sem=field_send.at[b, l],
                recv_sem=field_recv.at[b, l],
                device_id=((mem + k) % parts, me),
                device_id_type=MESH,
            ).start()

    for l in range(levels):
        share_field(0, l)
    loads[4].wait()
    for q in range(per_field):
        high, low = halves(b_all[:, q * width : (q + 1) * width])
        b_hi[q] = high
        b_lo[q] = low
    loads[6].wait()
    transposed = halves(a_all[...].T)
    at_hi[...], at_lo[...] = transposed
    k_hi[...], k_lo[...] = halves(product(halves(a_all[...]), transposed))
    loads[5].wait()

    def sent_strips(b, l):
        @pl.when(core == l)
        def _():
            bytes_of(strip.at[b, pl.ds(0, (strips // levels - 1) * rows)], t_send.at[b, l]).wait()

        @pl.when(core != l)
        def _():
            bytes_of(strip.at[b, pl.ds(0, strips // levels * rows)], t_send.at[b, l]).wait()

    def strips_of(b, l):
        bytes_of(field.at[b, l, pl.ds(0, parts - 1)], field_recv.at[b, l]).wait()
        for q in range(per_field):
            block = (members[:, l, :, q * width : (q + 1) * width] * field[b, l, q][None]).reshape(lines, width)
            high, low = halves(block)
            stack[:lines, q * width : (q + 1) * width] = high
            stack[lines:, q * width : (q + 1) * width] = low

        @pl.loop(0, per_field)
        def _(t):
            q = (my_part + t) % per_field
            t_out[b, l, q] = stacked_product(stack[...], (b_hi[q], b_lo[q]), NN)
            if l:

                @pl.when(t == 0)
                def _():
                    sent_strips(b, 0)

            @pl.loop(0, mem_dev)
            def _(k):
                m = (x + 6 - k // 2) % 4 * 2 + (z + k + 1) % 2
                d = strip_device(m, l, q)

                @pl.when(d != me)
                def _():
                    pltpu.make_async_remote_copy(
                        src_ref=t_out.at[b, l, q, pl.ds(m * rows, rows)],
                        dst_ref=strip.at[b, pl.ds(me * rows, rows)],
                        send_sem=t_send.at[b, l],
                        recv_sem=t_recv.at[b],
                        device_id=(mem, d),
                        device_id_type=MESH,
                    ).start()

                @pl.when(d == me)
                def _():
                    pltpu.make_async_copy(
                        t_out.at[b, l, q, pl.ds(m * rows, rows)], strip.at[b, pl.ds(me * rows, rows)], t_recv.at[b]
                    ).start()

    def to_rows(b, source, target, send, recv, pieces):
        mine = target.at[b, core, my_part, pl.ds(my_member * rows, rows)]
        for dx, piece in zip((2, 1, 3, 0), pieces):

            def send_one(k, dx=dx):
                d = (x + dx) % 4 * 16 + (z + k // 2 + 1) % 2 * 8 + (y + 6 - k // 4) % 4 * 2 + (core + k + 1) % 2
                pltpu.make_async_remote_copy(
                    src_ref=source.at[b, pl.ds(d * rows, rows)],
                    dst_ref=mine,
                    send_sem=send.at[b],
                    recv_sem=recv.at[b, core, my_part],
                    device_id=(mem, d),
                    device_id_type=MESH,
                ).start()

            if piece is not None:
                at = pl.ds((x + dx) % 4 * 16 * rows, 16 * rows)
                source[b, at] = piece(at)
            if dx:

                @pl.loop(0, 16)
                def _(k):
                    send_one(k)
            else:

                @pl.loop(0, 16)
                def _(k):
                    @pl.when(k != 11)
                    def _():
                        send_one(k)

        pltpu.make_async_copy(source.at[b, pl.ds(me * rows, rows)], mine, recv.at[b, core, my_part]).start()

    def mix(b):
        bytes_of(strip.at[b], t_recv.at[b]).wait()
        high, low = halves(strip[b])
        strip_hi[b] = high
        strip_lo[b] = low
        to_rows(
            b, mixed, mixed_rows, x_send, x_recv,
            [lambda at: product((k_hi[at], k_lo[at]), (high, low))] * 4,
        )

    def gradient_of(b):
        grad[b] = product((at_hi[...], at_lo[...]), (strip_hi[b], strip_lo[b]))

    def send_gradient(b):
        to_rows(b, grad, grad_rows, g_send, g_recv, [None] * 4)

    def part_of(b, l):
        for q in range(per_field):
            bytes_of(mixed_rows.at[b, l, q], x_recv.at[b, l, q]).wait()
            term = stacked_product(jnp.concatenate(halves(mixed_rows[b, l, q]), axis=0), (b_hi[q], b_lo[q]), NT)
            value[...] = term if q == 0 else value[...] + term
        for q in range(parts):
            shaped = value[:, q * width : (q + 1) * width].reshape(mem_dev, rows, width)
            part[b, l, q] = jnp.sum(members[:, l, :, q * width : (q + 1) * width] * shaped, axis=0)
        for k in range(1, parts):
            other = (mem + k) % parts
            pltpu.make_async_remote_copy(
                src_ref=part.at[b, l, other],
                dst_ref=got.at[b, l, mem],
                send_sem=part_send.at[b, l],
                recv_sem=part_recv.at[b, l],
                device_id=(other, me),
                device_id_type=MESH,
            ).start()
        got[b, l, mem] = part[b, l, mem]

    def image_of(b, l):
        bytes_of(got.at[b, l, pl.ds(0, parts - 1)], part_recv.at[b, l]).wait()
        image[b, l] = jnp.sum(got[b, l], axis=0)

    def lanes(x):
        return jnp.sum(x.reshape(-1, 8, 128), axis=0).sum(axis=0, keepdims=True)

    def start_round(b, n, slot, device):
        @pl.loop(1, parts * side)
        def _(k):
            pltpu.make_async_remote_copy(
                src_ref=sums.at[b, n],
                dst_ref=box.at[b, n, slot],
                send_sem=box_send.at[b, n],
                recv_sem=box_recv.at[b, n],
                device_id=device((slot + k) % (parts * side)),
                device_id_type=MESH,
            ).start()

        box[b, n, slot] = sums[b, n]

    def end_round(b, n):
        bytes_of(box.at[b, n, pl.ds(0, parts * side - 1)], box_recv.at[b, n]).wait()
        return jnp.sum(box[b, n], axis=0)

    def start_sums(b, norm, seen):
        row = lax.broadcasted_iota(jnp.int32, (8, 128), 0)
        sums[b, 0] = jnp.where(row == 0, lanes(norm), 0.0) + jnp.where(row == 1, lanes(seen), 0.0)
        start_round(b, 0, column, in_column)

    def pass_sums(b):
        sums[b, 1] = end_round(b, 0)
        start_round(b, 1, plane, in_plane)

    def end_sums(b):
        total = end_round(b, 1)
        norm = jnp.sum(total[0:1])
        return norm / (norm + jnp.sum(total[1:2]))

    def squares(x, w=None):
        y = x * x if w is None else x * x * w
        return (y[:, :128] + y[:, 128:]).reshape(-1, 8, 128)

    flat_weights = wfield[...].reshape(levels * rows, width)
    for l in range(levels):
        strips_of(0, l)
    mix(0)
    gradient_of(0)
    norm = squares(grad[0])
    for l in range(levels):
        part_of(0, l)
    for l in range(levels):
        image_of(0, l)
        field[1, l, mem] = wfield[l] * image[0, l]
        share_field(1, l)
    image0 = image[0]
    start_sums(0, norm, squares(image0.reshape(levels * rows, width), flat_weights))
    for l in range(levels):
        strips_of(1, l)
    mix(1)
    pass_sums(0)
    gradient_of(1)
    send_gradient(0)
    for l in range(levels):
        part_of(1, l)
    send_gradient(1)
    length0 = end_sums(0)
    keep = 1.0 - length0
    norm = squares(keep * grad[0] - length0 * grad[1])
    for l in range(levels):
        image_of(1, l)
    image1 = keep * image0 - length0 * image[1]
    start_sums(1, norm, squares(image1.reshape(levels * rows, width), flat_weights))
    pass_sums(1)
    length1 = end_sums(1)
    first = -(length0 + length1 * keep)
    second = length1 * length0
    increment[...] = first * image0 + second * image[1]
    for l in range(levels):
        for q in range(per_field):
            for b in range(2):
                bytes_of(grad_rows.at[b, l, q], g_recv.at[b, l, q]).wait()
            block = first * grad_rows[0, l, q] + second * grad_rows[1, l, q]
            control[:, l, :, q * width : (q + 1) * width] = block.reshape(mem_dev, rows, width)
    for b in range(2):
        sent = strip.at[b, pl.ds(0, nlat - rows)]
        bytes_of(sent, x_send.at[b]).wait()
        bytes_of(sent, g_send.at[b]).wait()
        sent_strips(b, 1)
        for l in range(levels):
            bytes_of(field.at[b, l, pl.ds(0, parts - 1)], field_send.at[b, l]).wait()
            bytes_of(field.at[b, l, pl.ds(0, parts - 1)], part_send.at[b, l]).wait()
        for n in range(2):
            bytes_of(box.at[b, n, pl.ds(0, parts * side - 1)], box_send.at[b, n]).wait()


def solution(mesh):
    parts, strips = mesh.shape["mem"], mesh.shape["lat"]

    def per_device(members, lat_root, lon_root, innovation, obs_weight, obs_mask, obs_cell):
        mem_dev, levels, rows, nlon = members.shape
        nlat = lat_root.shape[0]
        per_field = strips // (mem_dev * levels)
        width = nlon // per_field
        lines = mem_dev * rows
        vmem = pl.BlockSpec(memory_space=pltpu.VMEM)
        whole = pl.BlockSpec(memory_space=pltpu.HBM)
        slots = innovation.shape
        pair = pltpu.SemaphoreType.DMA((2,))
        levelled = pltpu.SemaphoreType.DMA((2, levels))
        quads = pltpu.SemaphoreType.DMA((2, levels, per_field))
        scratch = [
            pltpu.VMEM(members.shape, F32),
            *[pltpu.VMEM(slots, F32)] * 2,
            *[pltpu.VMEM(slots, jnp.int32)] * 2,
            pltpu.VMEM((nlat, nlat), F32),
            pltpu.VMEM((nlon, nlon), F32),
            *[pltpu.VMEM((nlat, nlat), BF16)] * 4,
            *[pltpu.VMEM((per_field, nlon, width), BF16)] * 2,
            pltpu.VMEM((2 * lines, nlon), BF16),
            pltpu.VMEM((2, levels, parts, rows, width), F32),
            pltpu.VMEM((levels, rows, width), F32),
            pltpu.VMEM((2, levels, per_field, lines, width), F32),
            pltpu.VMEM((2, nlat, width), F32),
            *[pltpu.VMEM((2, nlat, width), BF16)] * 2,
            *[pltpu.VMEM((2, nlat, width), F32)] * 2,
            *[pltpu.VMEM((2, levels, per_field, lines, width), F32)] * 2,
            pltpu.VMEM((lines, nlon), F32),
            *[pltpu.VMEM((2, levels, parts, rows, width), F32)] * 2,
            pltpu.VMEM((2, levels, rows, width), F32),
            pltpu.VMEM((2, 2, 8, 128), F32),
            pltpu.VMEM((2, 2, 16, 8, 128), F32),
            pltpu.SemaphoreType.DMA((7,)),
            levelled, levelled, levelled, pair,
            pair, quads, pair, quads,
            levelled, levelled,
            *[pltpu.SemaphoreType.DMA((2, 2))] * 2,
        ]
        return pl.pallas_call(
            kernel,
            out_shape=(
                jax.ShapeDtypeStruct((levels, rows, nlon // parts), F32),
                jax.ShapeDtypeStruct(members.shape, F32),
            ),
            in_specs=[whole] * 7,
            out_specs=(vmem, vmem),
            scratch_shapes=scratch,
            compiler_params=pltpu.CompilerParams(
                collective_id=0, has_side_effects=True, vmem_limit_bytes=62 * 1024 * 1024
            ),
            cost_estimate=pl.CostEstimate(flops=5_000_000_000, bytes_accessed=7_000_000, transcendentals=0),
        )(members, lat_root, lon_root, innovation, obs_weight, obs_mask, obs_cell)

    return jax.shard_map(
        per_device,
        mesh=mesh,
        in_specs=(P("mem", None, "lat", None), P(), P(), *[P("lat", "mem")] * 4),
        out_specs=(P(None, "lat", "mem"), P("mem", None, "lat", None)),
        check_vma=False,
    )
```

time: 109 us -> 90.5 us (0.83)
  Pallas kernels: 101 us -> 86.4 us
  local copies, waits for them, and re-layouts: 6.4 us -> 3.21 us
    pallas_call x1, Pallas kernels: 101 us -> 86.4 us  [per_device(): pl.pallas_call(kernel, out_shape=(jax.ShapeDtypeStruct((levels, rows, nlo...]
    unnamed x14 -> x2, local copies, waits for them, and re-layouts: 6.4 us -> 3.21 us
where the time goes in v3:
time: 90.5 us; the launch traced here: 90.3 us
  Pallas kernels  86.4 us (95%)
  local copies, waits for them, and re-layouts  3.21 us (4%)
    pallas_call x1, Pallas kernels, per_device(): pl.pallas_call(kernel, out_shape=(jax.ShapeDtypeStruct((levels, rows, nlo...  86.4 us
    unnamed x2, local copies, waits for them, and re-layouts  3.21 us

profile of v3, /device:TPU:1, one launch (start us, length us, event | category | flops | bytes accessed | tf_op | source)
XLA Modules:
  0.0 90.3 jit_solution(1986156273273856644)
XLA Ops:
  0.6 86.4 %shard_map.86 = (f32[2,8,256]{2,1,0:T(8,128)}, f32[8,2,8,1024]{3,2,1,0:T(8,128)}) custom-call(f32[8,2,8,1024]{3,2,1,0:T(8,128)} %members_hbm.1, f32[512,512]{1,0:T(8,128)} %a_hbm.1, f32[1024,1024]{1,0:T(8,128)} %b_hbm.1, f32[8,64]{1,0:T(8,128)} %innovation_hbm.1, f32[8,64]{1,0:T(8,128)} %weight_hbm.1, s32[8,64]{1,0:T(8,128)} %mask_hbm.1, s32[8,64]{1,0:T(8,128)} %cell_hbm.1), custom_call_target="tpu_custom_call" | custom-call | flops 5000000000 | bytes 7000000 | tf_op jit(solution)/shard_map/pallas_call | solution.py:392
  87.1 1.3 %copy.11 = f32[2,8,256]{2,1,0:T(8,128)} copy(f32[2,8,256]{2,1,0:T(8,128)} %get-tuple-element.4) | data formatting | bytes 32768
  88.4 1.9 %copy.12 = f32[8,2,8,1024]{3,2,1,0:T(8,128)} copy(f32[8,2,8,1024]{3,2,1,0:T(8,128)} %get-tuple-element.5) | data formatting | bytes 1048576

commit v4 on v3

--- a/solution.py
+++ b/solution.py
@@ -36,8 +36,8 @@
     increment, control,
     members, innovation, obs_weight, obs_mask, obs_cell, a_all, b_all, k_hi, k_lo, at_hi, at_lo, b_hi, b_lo, stack,
     field, wfield, t_out, strip, strip_hi, strip_lo, grad, mixed, mixed_rows, grad_rows, value,
-    part, got, image, sums, box,
-    load_sem, field_send, field_recv, t_send, t_recv, x_send, x_recv, g_send, g_recv,
+    part, got, all_parts, image, sums, box,
+    load_sem, w_send, w_recv, field_send, field_recv, t_send, t_recv, x_send, x_recv, g_send, g_recv,
     part_send, part_recv, box_send, box_recv,
 ):
     mem_dev, levels, rows, nlon = members.shape
@@ -72,9 +72,6 @@
             (b_hbm, b_all), (members_hbm, members), (a_hbm, a_all),
         ])
     ]
-    for load in loads:
-        load.start()
-
     barrier = pltpu.get_barrier_semaphore()
 
     @pl.loop(1, strips)
@@ -87,6 +84,8 @@
         def _():
             pl.semaphore_signal(barrier, inc=1, device_id=in_column(k), device_id_type=MESH)
 
+    for load in loads:
+        load.start()
     for load in loads[:4]:
         load.wait()
     weights = obs_weight[...] * obs_mask[...].astype(F32)
@@ -101,7 +100,7 @@
         wsum = wsum + jnp.where(hit, weights[:, j : j + 1], 0.0)
         hsum = hsum + jnp.where(hit, pulled[:, j : j + 1], 0.0)
     for l in range(levels):
-        wfield[l] = wsum[:, l * width : (l + 1) * width]
+        wfield[l, mem] = wsum[:, l * width : (l + 1) * width]
         field[0, l, mem] = hsum[:, l * width : (l + 1) * width]
 
     pl.semaphore_wait(barrier, strips - 1 + (parts - 1) * side)
@@ -109,19 +108,20 @@
     def bytes_of(ref, sem):
         return pltpu.make_async_copy(ref, ref, sem)
 
-    def share_field(b, l):
+    def to_column(source, target, send, recv):
         for k in range(1, parts):
             pltpu.make_async_remote_copy(
-                src_ref=field.at[b, l, mem],
-                dst_ref=field.at[b, l, mem],
-                send_sem=field_send.at[b, l],
-                recv_sem=field_recv.at[b, l],
+                src_ref=source,
+                dst_ref=target,
+                send_sem=send,
+                recv_sem=recv,
                 device_id=((mem + k) % parts, me),
                 device_id_type=MESH,
             ).start()
 
     for l in range(levels):
-        share_field(0, l)
+        to_column(field.at[0, l, mem], field.at[0, l, mem], field_send.at[0, l], field_recv.at[0, l])
+    to_column(wfield.at[:, mem], wfield.at[:, mem], w_send.at[0], w_recv.at[0])
     loads[4].wait()
     for q in range(per_field):
         high, low = halves(b_all[:, q * width : (q + 1) * width])
@@ -143,7 +143,8 @@
             bytes_of(strip.at[b, pl.ds(0, strips // levels * rows)], t_send.at[b, l]).wait()
 
     def strips_of(b, l):
-        bytes_of(field.at[b, l, pl.ds(0, parts - 1)], field_recv.at[b, l]).wait()
+        if b == 0:
+            bytes_of(field.at[0, l, pl.ds(0, parts - 1)], field_recv.at[0, l]).wait()
         for q in range(per_field):
             block = (members[:, l, :, q * width : (q + 1) * width] * field[b, l, q][None]).reshape(lines, width)
             high, low = halves(block)
@@ -239,6 +240,10 @@
         for q in range(parts):
             shaped = value[:, q * width : (q + 1) * width].reshape(mem_dev, rows, width)
             part[b, l, q] = jnp.sum(members[:, l, :, q * width : (q + 1) * width] * shaped, axis=0)
+        if b == 0:
+            to_column(part.at[0, l], all_parts.at[l, mem], part_send.at[0, l], part_recv.at[0, l])
+            all_parts[l, mem] = part[0, l]
+            return
         for k in range(1, parts):
             other = (mem + k) % parts
             pltpu.make_async_remote_copy(
@@ -252,6 +257,13 @@
         got[b, l, mem] = part[b, l, mem]
 
     def image_of(b, l):
+        if b == 0:
+            bytes_of(all_parts.at[l, pl.ds(0, parts - 1)], part_recv.at[0, l]).wait()
+            for q in range(parts):
+                whole = jnp.sum(all_parts[l, :, q], axis=0)
+                field[1, l, q] = wfield[l, q] * whole
+            image[0, l] = jnp.sum(all_parts[l, :, mem], axis=0)
+            return
         bytes_of(got.at[b, l, pl.ds(0, parts - 1)], part_recv.at[b, l]).wait()
         image[b, l] = jnp.sum(got[b, l], axis=0)
 
@@ -294,7 +306,6 @@
         y = x * x if w is None else x * x * w
         return (y[:, :128] + y[:, 128:]).reshape(-1, 8, 128)
 
-    flat_weights = wfield[...].reshape(levels * rows, width)
     for l in range(levels):
         strips_of(0, l)
     mix(0)
@@ -302,14 +313,14 @@
     norm = squares(grad[0])
     for l in range(levels):
         part_of(0, l)
-    for l in range(levels):
-        image_of(0, l)
-        field[1, l, mem] = wfield[l] * image[0, l]
-        share_field(1, l)
+    bytes_of(mixed.at[0, pl.ds(0, (parts - 1) * levels * rows)], w_recv.at[0]).wait()
+    image_of(0, 0)
+    strips_of(1, 0)
+    image_of(0, 1)
+    flat_weights = wfield[:, mem].reshape(levels * rows, width)
     image0 = image[0]
     start_sums(0, norm, squares(image0.reshape(levels * rows, width), flat_weights))
-    for l in range(levels):
-        strips_of(1, l)
+    strips_of(1, 1)
     mix(1)
     pass_sums(0)
     gradient_of(1)
@@ -335,14 +346,18 @@
                 bytes_of(grad_rows.at[b, l, q], g_recv.at[b, l, q]).wait()
             block = first * grad_rows[0, l, q] + second * grad_rows[1, l, q]
             control[:, l, :, q * width : (q + 1) * width] = block.reshape(mem_dev, rows, width)
+    bytes_of(mixed.at[0, pl.ds(0, (parts - 1) * levels * rows)], w_send.at[0]).wait()
     for b in range(2):
         sent = strip.at[b, pl.ds(0, nlat - rows)]
         bytes_of(sent, x_send.at[b]).wait()
         bytes_of(sent, g_send.at[b]).wait()
         sent_strips(b, 1)
         for l in range(levels):
-            bytes_of(field.at[b, l, pl.ds(0, parts - 1)], field_send.at[b, l]).wait()
-            bytes_of(field.at[b, l, pl.ds(0, parts - 1)], part_send.at[b, l]).wait()
+            if b == 0:
+                bytes_of(field.at[0, l, pl.ds(0, parts - 1)], field_send.at[0, l]).wait()
+                bytes_of(all_parts.at[l, pl.ds(0, parts - 1)], part_send.at[0, l]).wait()
+            else:
+                bytes_of(field.at[b, l, pl.ds(0, parts - 1)], part_send.at[b, l]).wait()
         for n in range(2):
             bytes_of(box.at[b, n, pl.ds(0, parts * side - 1)], box_send.at[b, n]).wait()
 
@@ -372,7 +387,7 @@
             *[pltpu.VMEM((per_field, nlon, width), BF16)] * 2,
             pltpu.VMEM((2 * lines, nlon), BF16),
             pltpu.VMEM((2, levels, parts, rows, width), F32),
-            pltpu.VMEM((levels, rows, width), F32),
+            pltpu.VMEM((levels, parts, rows, width), F32),
             pltpu.VMEM((2, levels, per_field, lines, width), F32),
             pltpu.VMEM((2, nlat, width), F32),
             *[pltpu.VMEM((2, nlat, width), BF16)] * 2,
@@ -380,10 +395,12 @@
             *[pltpu.VMEM((2, levels, per_field, lines, width), F32)] * 2,
             pltpu.VMEM((lines, nlon), F32),
             *[pltpu.VMEM((2, levels, parts, rows, width), F32)] * 2,
+            pltpu.VMEM((levels, parts, parts, rows, width), F32),
             pltpu.VMEM((2, levels, rows, width), F32),
             pltpu.VMEM((2, 2, 8, 128), F32),
             pltpu.VMEM((2, 2, 16, 8, 128), F32),
             pltpu.SemaphoreType.DMA((7,)),
+            *[pltpu.SemaphoreType.DMA((1,))] * 2,
             levelled, levelled, levelled, pair,
             pair, quads, pair, quads,
             levelled, levelled,

time: 90.5 us -> 88.6 us (0.979)
  Pallas kernels: 86.4 us -> 84.6 us
    pallas_call x1, Pallas kernels: 86.4 us -> 84.6 us  [per_device(): pl.pallas_call(kernel, out_shape=(jax.ShapeDtypeStruct((levels, rows, nlo...]
where the time goes in v4:
time: 88.6 us; the launch traced here: 88.4 us
  Pallas kernels  84.6 us (95%)
  local copies, waits for them, and re-layouts  3.21 us (4%)
    pallas_call x1, Pallas kernels, per_device(): pl.pallas_call(kernel, out_shape=(jax.ShapeDtypeStruct((levels, rows, nlo...  84.6 us
    unnamed x2, local copies, waits for them, and re-layouts  3.21 us

profile of v4, /device:TPU:1, one launch (start us, length us, event | category | flops | bytes accessed | tf_op | source)
XLA Modules:
  0.0 88.4 jit_solution(16180850455518485336)
XLA Ops:
  0.6 84.6 %shard_map.86 = (f32[2,8,256]{2,1,0:T(8,128)}, f32[8,2,8,1024]{3,2,1,0:T(8,128)}) custom-call(f32[8,2,8,1024]{3,2,1,0:T(8,128)} %members_hbm.1, f32[512,512]{1,0:T(8,128)} %a_hbm.1, f32[1024,1024]{1,0:T(8,128)} %b_hbm.1, f32[8,64]{1,0:T(8,128)} %innovation_hbm.1, f32[8,64]{1,0:T(8,128)} %weight_hbm.1, s32[8,64]{1,0:T(8,128)} %mask_hbm.1, s32[8,64]{1,0:T(8,128)} %cell_hbm.1), custom_call_target="tpu_custom_call" | custom-call | flops 5000000000 | bytes 7000000 | tf_op jit(solution)/shard_map/pallas_call | solution.py:409
  85.2 1.3 %copy.11 = f32[2,8,256]{2,1,0:T(8,128)} copy(f32[2,8,256]{2,1,0:T(8,128)} %get-tuple-element.4) | data formatting | bytes 32768
  86.5 1.9 %copy.12 = f32[8,2,8,1024]{3,2,1,0:T(8,128)} copy(f32[8,2,8,1024]{3,2,1,0:T(8,128)} %get-tuple-element.5) | data formatting | bytes 1048576

commit v5 on v4

--- a/solution.py
+++ b/solution.py
@@ -121,7 +121,6 @@
 
     for l in range(levels):
         to_column(field.at[0, l, mem], field.at[0, l, mem], field_send.at[0, l], field_recv.at[0, l])
-    to_column(wfield.at[:, mem], wfield.at[:, mem], w_send.at[0], w_recv.at[0])
     loads[4].wait()
     for q in range(per_field):
         high, low = halves(b_all[:, q * width : (q + 1) * width])
@@ -155,11 +154,10 @@
         def _(t):
             q = (my_part + t) % per_field
             t_out[b, l, q] = stacked_product(stack[...], (b_hi[q], b_lo[q]), NN)
-            if l:
-
-                @pl.when(t == 0)
-                def _():
-                    sent_strips(b, 0)
+
+            @pl.when((l > 0) & (t == 0))
+            def _():
+                sent_strips(b, 0)
 
             @pl.loop(0, mem_dev)
             def _(k):
@@ -233,10 +231,13 @@
         to_rows(b, grad, grad_rows, g_send, g_recv, [None] * 4)
 
     def part_of(b, l):
-        for q in range(per_field):
+        value[...] = jnp.zeros_like(value)
+
+        @pl.loop(0, per_field)
+        def _(q):
             bytes_of(mixed_rows.at[b, l, q], x_recv.at[b, l, q]).wait()
-            term = stacked_product(jnp.concatenate(halves(mixed_rows[b, l, q]), axis=0), (b_hi[q], b_lo[q]), NT)
-            value[...] = term if q == 0 else value[...] + term
+            value[...] += stacked_product(jnp.concatenate(halves(mixed_rows[b, l, q]), axis=0), (b_hi[q], b_lo[q]), NT)
+
         for q in range(parts):
             shaped = value[:, q * width : (q + 1) * width].reshape(mem_dev, rows, width)
             part[b, l, q] = jnp.sum(members[:, l, :, q * width : (q + 1) * width] * shaped, axis=0)
@@ -306,27 +307,39 @@
         y = x * x if w is None else x * x * w
         return (y[:, :128] + y[:, 128:]).reshape(-1, 8, 128)
 
-    for l in range(levels):
+
+    @pl.loop(0, levels)
+    def _(l):
         strips_of(0, l)
+
+    to_column(wfield.at[:, mem], wfield.at[:, mem], w_send.at[0], w_recv.at[0])
     mix(0)
     gradient_of(0)
     norm = squares(grad[0])
-    for l in range(levels):
+
+    @pl.loop(0, levels)
+    def _(l):
         part_of(0, l)
+
     bytes_of(mixed.at[0, pl.ds(0, (parts - 1) * levels * rows)], w_recv.at[0]).wait()
-    image_of(0, 0)
-    strips_of(1, 0)
-    image_of(0, 1)
+
+    @pl.loop(0, levels)
+    def _(l):
+        image_of(0, l)
+        strips_of(1, l)
+
     flat_weights = wfield[:, mem].reshape(levels * rows, width)
     image0 = image[0]
     start_sums(0, norm, squares(image0.reshape(levels * rows, width), flat_weights))
-    strips_of(1, 1)
     mix(1)
     pass_sums(0)
     gradient_of(1)
     send_gradient(0)
-    for l in range(levels):
+
+    @pl.loop(0, levels)
+    def _(l):
         part_of(1, l)
+
     send_gradient(1)
     length0 = end_sums(0)
     keep = 1.0 - length0

time: 88.6 us -> 87.7 us (0.990)
  Pallas kernels: 84.6 us -> 83.6 us
    pallas_call x1, Pallas kernels: 84.6 us -> 83.6 us  [per_device(): pl.pallas_call(kernel, out_shape=(jax.ShapeDtypeStruct((levels, rows, nlo...]
where the time goes in v5:
time: 87.7 us; the launch traced here: 87.5 us
  Pallas kernels  83.6 us (95%)
  local copies, waits for them, and re-layouts  3.21 us (4%)
    pallas_call x1, Pallas kernels, per_device(): pl.pallas_call(kernel, out_shape=(jax.ShapeDtypeStruct((levels, rows, nlo...  83.6 us
    unnamed x2, local copies, waits for them, and re-layouts  3.21 us

profile of v5, /device:TPU:1, one launch (start us, length us, event | category | flops | bytes accessed | tf_op | source)
XLA Modules:
  0.0 87.5 jit_solution(1493954287664884305)
XLA Ops:
  0.6 83.6 %shard_map.86 = (f32[2,8,256]{2,1,0:T(8,128)}, f32[8,2,8,1024]{3,2,1,0:T(8,128)}) custom-call(f32[8,2,8,1024]{3,2,1,0:T(8,128)} %members_hbm.1, f32[512,512]{1,0:T(8,128)} %a_hbm.1, f32[1024,1024]{1,0:T(8,128)} %b_hbm.1, f32[8,64]{1,0:T(8,128)} %innovation_hbm.1, f32[8,64]{1,0:T(8,128)} %weight_hbm.1, s32[8,64]{1,0:T(8,128)} %mask_hbm.1, s32[8,64]{1,0:T(8,128)} %cell_hbm.1), custom_call_target="tpu_custom_call" | custom-call | flops 5000000000 | bytes 7000000 | tf_op jit(solution)/shard_map/pallas_call | solution.py:422
  84.3 1.3 %copy.11 = f32[2,8,256]{2,1,0:T(8,128)} copy(f32[2,8,256]{2,1,0:T(8,128)} %get-tuple-element.4) | data formatting | bytes 32768
  85.6 1.9 %copy.12 = f32[8,2,8,1024]{3,2,1,0:T(8,128)} copy(f32[8,2,8,1024]{3,2,1,0:T(8,128)} %get-tuple-element.5) | data formatting | bytes 1048576

commit v6 on v5

--- a/solution.py
+++ b/solution.py
@@ -155,9 +155,11 @@
             q = (my_part + t) % per_field
             t_out[b, l, q] = stacked_product(stack[...], (b_hi[q], b_lo[q]), NN)
 
-            @pl.when((l > 0) & (t == 0))
-            def _():
-                sent_strips(b, 0)
+            if b == 0:
+
+                @pl.when((l > 0) & (t == 0))
+                def _():
+                    sent_strips(b, 0)
 
             @pl.loop(0, mem_dev)
             def _(k):
@@ -364,6 +366,8 @@
         sent = strip.at[b, pl.ds(0, nlat - rows)]
         bytes_of(sent, x_send.at[b]).wait()
         bytes_of(sent, g_send.at[b]).wait()
+        if b == 1:
+            sent_strips(b, 0)
         sent_strips(b, 1)
         for l in range(levels):
             if b == 0:

time: 87.7 us -> 87.3 us (level)
  no operation moved by 1% of the time
where the time goes in v6:
time: 87.3 us; the launch traced here: 87.1 us
  Pallas kernels  83.3 us (95%)
  local copies, waits for them, and re-layouts  3.21 us (4%)
    pallas_call x1, Pallas kernels, per_device(): pl.pallas_call(kernel, out_shape=(jax.ShapeDtypeStruct((levels, rows, nlo...  83.3 us
    unnamed x2, local copies, waits for them, and re-layouts  3.21 us

profile of v6, /device:TPU:1, one launch (start us, length us, event | category | flops | bytes accessed | tf_op | source)
XLA Modules:
  0.0 87.1 jit_solution(8182034232834751564)
XLA Ops:
  0.6 83.3 %shard_map.86 = (f32[2,8,256]{2,1,0:T(8,128)}, f32[8,2,8,1024]{3,2,1,0:T(8,128)}) custom-call(f32[8,2,8,1024]{3,2,1,0:T(8,128)} %members_hbm.1, f32[512,512]{1,0:T(8,128)} %a_hbm.1, f32[1024,1024]{1,0:T(8,128)} %b_hbm.1, f32[8,64]{1,0:T(8,128)} %innovation_hbm.1, f32[8,64]{1,0:T(8,128)} %weight_hbm.1, s32[8,64]{1,0:T(8,128)} %mask_hbm.1, s32[8,64]{1,0:T(8,128)} %cell_hbm.1), custom_call_target="tpu_custom_call" | custom-call | flops 5000000000 | bytes 7000000 | tf_op jit(solution)/shard_map/pallas_call | solution.py:426
  83.9 1.3 %copy.11 = f32[2,8,256]{2,1,0:T(8,128)} copy(f32[2,8,256]{2,1,0:T(8,128)} %get-tuple-element.4) | data formatting | bytes 32768
  85.2 1.9 %copy.12 = f32[8,2,8,1024]{3,2,1,0:T(8,128)} copy(f32[8,2,8,1024]{3,2,1,0:T(8,128)} %get-tuple-element.5) | data formatting | bytes 1048576
